TPU v7x, 256 devices: a whole 4x4x8 slice. The times are simulated.
256 devices in a mesh: row: 64 (over y, z, core), col: 4 (over x).
Axes of the slice: x: 4, y: 4, z: 8, core: 2. Of those that a mesh axis runs over, the one named last changes fastest.
Arguments:
- queries: bfloat16 [32768, 256], P(('row', 'col')), may hold values from -10 to 10, as said below
- candidates: bfloat16 [32768, 256], P(('row', 'col')), may hold values from -10 to 10, as said below
- block_mask: int32 [256, 256], replicated, may hold values 0 or 1
- row_class: int32 [32768], replicated, may hold values from 0 to 7
- col_class: int32 [32768], replicated, may hold values from 0 to 7
- cotangent: float32 [32768], P('row'), may hold values from -6 to 6
Outputs:
- query_grads: float32 [32768, 256], P(('row', 'col'))
- candidate_grads: float32 [32768, 256], P(('row', 'col'))
Inputs may be any that keep to these rules, and one draw needn't show every extreme that they name: `queries`: one embedding a session. `candidates`: one embedding a session.
All inputs are finite; a program needn't handle non-finite values.
Results may differ from a plain program's by a relative error of at most 0.004.
Values may be sent and summed in bfloat16 or wider, within the bound.
A program may use at most 128 MiB of HBM per device.

v0:
```python
import math

import jax
import jax.numpy as jnp
from jax import lax
from jax.sharding import PartitionSpec as P

BLOCK = 128


def joined(part, axis, combine):
    gathered = jax.tree.map(lambda a: lax.all_gather(a, axis), part)

    def take(source):
        return jax.tree.map(lambda a: lax.dynamic_index_in_dim(a, source, 0, False), gathered)

    return lax.fori_loop(
        1, lax.axis_size(axis), lambda source, state: combine(state, take(source)), take(0)
    )


def one_hot_blocks(ids, n_blocks):
    return ((ids // BLOCK)[:, None] == jnp.arange(n_blocks, dtype=jnp.int32)[None, :]).astype(
        jnp.bfloat16
    )


def block_picks(col_ids, block_mask):
    n_blocks = block_mask.shape[0]
    return lax.dot_general(
        one_hot_blocks(col_ids, n_blocks),
        block_mask.astype(jnp.bfloat16),
        (((1,), (1,)), ((), ())),
        preferred_element_type=jnp.float32,
    ).astype(jnp.bfloat16)


def hit_table(picks, col_labels, row_ids, row_labels):
    n_blocks = picks.shape[1]
    block_hits = lax.dot_general(
        picks,
        one_hot_blocks(row_ids, n_blocks),
        (((1,), (1,)), ((), ())),
        preferred_element_type=jnp.float32,
    )
    same_class = col_labels[:, None] == row_labels[None, :]
    return jnp.where((block_hits > 0.5) & same_class, 1.0, 0.0).astype(jnp.bfloat16)


def join_two(first, second):
    top = jnp.maximum(first[0], second[0])
    return (top, first[1] * jnp.exp(first[0] - top) + second[1] * jnp.exp(second[0] - top))


def join_three(first, second):
    top, mass = join_two(first, second)
    return (top, mass, first[2] + second[2])


def shards(queries, candidates, block_mask, row_class, col_class, cotangent):
    rows_dev = queries.shape[0]
    width = queries.shape[1]
    scale = 1.0 / math.sqrt(width)
    n_col = lax.axis_size("col")
    row_pos = lax.axis_index("row")
    col_pos = lax.axis_index("col")
    query_rows = lax.all_gather(queries, "col", axis=0, tiled=True)
    cand_rows = lax.all_gather(candidates, "row", axis=0, tiled=True)
    n_rows = query_rows.shape[0]
    n_cands = cand_rows.shape[0]
    row_start = row_pos * n_rows
    row_ids = row_start + jnp.arange(n_rows, dtype=jnp.int32)
    row_labels = lax.dynamic_slice_in_dim(row_class, row_start, n_rows, 0)
    places = jnp.arange(n_cands, dtype=jnp.int32)
    col_ids = (places // rows_dev * n_col + col_pos) * rows_dev + places % rows_dev
    col_labels = lax.dynamic_slice_in_dim(
        col_class.reshape(-1, n_col, rows_dev), col_pos, 1, 1
    ).reshape(n_cands)
    hits_all = hit_table(block_picks(col_ids, block_mask), col_labels, row_ids, row_labels)
    span = math.gcd(n_cands, 2048)
    blocks = n_cands // span
    cand_blocks = cand_rows.reshape(blocks, span, width)
    hit_blocks = hits_all.reshape(blocks, span, n_rows)

    def scores_of(cand_block):
        return (
            lax.dot_general(
                cand_block, query_rows, (((1,), (1,)), ((), ())), preferred_element_type=jnp.float32
            )
            * scale
        )

    def gather_stats(carry, inputs):
        scores = scores_of(inputs[0])
        block_max = jnp.max(scores, axis=0)
        block_mass = jnp.sum(jnp.exp(scores - block_max), axis=0)
        block_count = jnp.sum(inputs[1].astype(jnp.float32), axis=0)
        return (join_three(carry, (block_max, block_mass, block_count)), None)

    start_stats = (
        jnp.full((n_rows,), -jnp.inf, jnp.float32),
        jnp.zeros((n_rows,), jnp.float32),
        jnp.zeros((n_rows,), jnp.float32),
    )
    (row_max, row_mass, row_count), unused = lax.scan(
        gather_stats, start_stats, (cand_blocks, hit_blocks)
    )
    row_max, row_mass = joined((row_max, row_mass), "col", join_two)
    row_count = lax.psum(row_count, "col")
    row_lse = row_max + jnp.log(row_mass)
    denom = jnp.maximum(row_count, 1.0)
    coef_soft = cotangent * row_count / denom
    coef_pos = cotangent / denom

    def grad_block(total, inputs):
        scores = scores_of(inputs[0])
        grads = (
            coef_soft * jnp.exp(scores - row_lse) - coef_pos * inputs[1].astype(jnp.float32)
        ).astype(jnp.bfloat16)
        total = total + lax.dot_general(
            grads, inputs[0], (((0,), (0,)), ((), ())), preferred_element_type=jnp.float32
        )
        return (total, grads)

    query_term, grad_blocks = lax.scan(
        grad_block, jnp.zeros((n_rows, width), jnp.float32), (cand_blocks, hit_blocks)
    )
    query_grads = lax.psum_scatter(query_term, "col", scatter_dimension=0, tiled=True) * scale
    grad_table = grad_blocks.reshape(n_cands, n_rows)
    cand_total = lax.psum_scatter(
        jnp.dot(grad_table, query_rows, preferred_element_type=jnp.float32),
        "row",
        scatter_dimension=0,
        tiled=True,
    )
    return (query_grads, cand_total * scale)


def solution(mesh):
    in_specs = (P(("row", "col"), None), P(("row", "col"), None), P(), P(), P(), P("row"))
    out_specs = (P(("row", "col"), None), P(("row", "col"), None))
    return jax.shard_map(shards, mesh=mesh, in_specs=in_specs, out_specs=out_specs, check_vma=False)
```

profile of v0, /device:TPU:1, one launch (start us, length us, event | category | flops | bytes accessed | tf_op | source)
XLA Modules:
  0.0 348.2 jit_solution(3944083704085497390)
XLA Ops:
  8.0 0.8 dynamic_slice.48
  8.8 11.2 %all_gather.19 = bf16[512,256]{1,0:T(8,128)(2,1)S(1)} all-gather(bf16[128,256]{1,0:T(8,128)(2,1)} %param.12), channel_id=1, replica_groups=mesh['row'=64,'col'=4] {'col'}, dimensions={0}, use_global_device_ids=true | all-gather | bytes 327680 | tf_op jit(solution)/shard_map/all_gather | solution.py:67
  20.1 7.2 %select_convert_fusion = bf16[8192,512]{1,0:T(8,128)(2,1)} fusion(s32[512]{0:T(512)S(1)} %dynamic_slice.48, s32[8192]{0:T(1024)S(1)} %bitcast.69, s32[8192]{0:T(1024)S(1)} %add_select_fusion, s32[512]{0:T(512)S(1)} %add_select_fusion.2, s32[256,256]{1,0:T(8,128)} %param.14), kind=kOutput, calls=%fused_computation.25 | convolution fusion | flops 3246587904 | bytes 8720384 | tf_op jit(solution)/shard_map/dot_general | solution.py:40
  27.3 66.8 %all-gather.6.cloned.1.call-done = bf16[8192,256]{1,0:T(8,128)(2,1)} async-done(((bf16[128,256]{1,0:T(8,128)(2,1)}), bf16[8192,256]{1,0:T(8,128)(2,1)}) %all-gather.6.cloned.1.call-update) | async-done | bytes 4194320 | tf_op jit(solution)/shard_map/all_gather | solution.py:68
  94.1 18.8 %while.46 = (s32[]{:T(128)}, f32[512]{0:T(512)S(1)}, f32[512]{0:T(512)S(1)}, f32[512]{0:T(512)S(1)}, bf16[4,2048,256]{2,1,0:T(8,128)(2,1)}, /*index=5*/bf16[512,...) while((s32[]{:T(128)}, f32[512]{0:T(512)S(1)}, f32[512]{0:T(512)S(1)}, ...), condition=%wide.region_4.5_spmd.clone, body=%wide.region_0.4_spmd.clone.sunk | while | flops 544214528 | bytes 11823723 | solution.py:105
  94.1 2.0 multiply_reduce_fusion.2
  96.8 1.9 convert_reduce_fusion.2
  98.8 2.0 multiply_reduce_fusion.2
  100.8 0.8 exponential_reduce_fusion.2
  101.6 1.9 convert_reduce_fusion.2
  103.5 2.0 multiply_reduce_fusion.2
  106.3 1.9 convert_reduce_fusion.2
  108.2 2.0 multiply_reduce_fusion.2
  111.0 1.9 convert_reduce_fusion.2
  112.9 8.4 %all-gather.2 = f32[4,1,512]{2,1,0:T(1,128)S(1)} all-gather(f32[1,1,512]{2,1,0:T(1,128)S(1)} %bitcast.65), channel_id=2, replica_groups=mesh['row'=64,'col'=4] {'col'}, dimensions={0}, use_global_device_ids=true | all-gather | bytes 10240 | tf_op jit(solution)/shard_map/all_gather | solution.py:12
  121.3 8.1 %all-gather.3 = f32[4,1,512]{2,1,0:T(1,128)S(1)} all-gather(f32[1,1,512]{2,1,0:T(1,128)S(1)} %bitcast.66), channel_id=3, replica_groups=mesh['row'=64,'col'=4] {'col'}, dimensions={0}, use_global_device_ids=true | all-gather | bytes 10240 | tf_op jit(solution)/shard_map/all_gather | solution.py:12
  129.6 6.4 %psum.7 = f32[512]{0:T(512)S(1)} all-reduce(f32[512]{0:T(512)S(1)} %get-tuple-element.222), channel_id=1, replica_groups=mesh['row'=64,'col'=4] {'col'}, use_global_device_ids=true, to_apply=%region_7.8 | all-reduce | flops 512 | bytes 4096 | tf_op jit(solution)/shard_map/psum | solution.py:109
  136.0 26.7 %while.47 = (s32[]{:T(128)}, f32[512,256]{1,0:T(8,128)S(1)}, bf16[4,2048,512]{2,1,0:T(8,128)(2,1)}, f32[512]{0:T(512)S(1)}, bf16[4,2048,256]{2,1,0:T(8,128)(2,1)...) while((s32[]{:T(128)}, f32[512,256]{1,0:T(8,128)S(1)}, ...), condition=%wide.region_9.10_spmd.clone, body=%wide.region_8.9_spmd.clone.sunk | while | flops 1081344000 | bytes 11804279 | solution.py:125
  136.0 4.6 %bitcast_dynamic-update-slice_fusion.2 = (bf16[4,2048,512]{2,1,0:T(8,128)(2,1)}, bf16[2048,512]{1,0:T(8,128)(2,1)S(1)}) fusion(bf16[4,2048,512]{2,1,0:T(8,128)(2,1)} %get-tuple-element.553, s32[]{:T(128)} %get-tuple-element.551, bf16[4,2048,512]{2,1,0:T(8,128)(2,1)} %get-tuple-element.570, f32[512]{0:T(512)S(1)} %get-tuple-element.569, ...), kind=kOutput, calls=%fused_computation.17.clone.1 | convolution fusion | flops 544210944 | bytes 7609344 | tf_op jit(solution)/shard_map/while/body/eval_jaxpr/dot_general | solution.py:87
  140.6 2.1 convolution_add_fusion.2
  142.7 4.6 %bitcast_dynamic-update-slice_fusion.2 = (bf16[4,2048,512]{2,1,0:T(8,128)(2,1)}, bf16[2048,512]{1,0:T(8,128)(2,1)S(1)}) fusion(bf16[4,2048,512]{2,1,0:T(8,128)(2,1)} %get-tuple-element.553, s32[]{:T(128)} %get-tuple-element.551, bf16[4,2048,512]{2,1,0:T(8,128)(2,1)} %get-tuple-element.570, f32[512]{0:T(512)S(1)} %get-tuple-element.569, ...), kind=kOutput, calls=%fused_computation.17.clone.1 | convolution fusion | flops 544210944 | bytes 7609344 | tf_op jit(solution)/shard_map/while/body/eval_jaxpr/dot_general | solution.py:87
  147.3 2.1 convolution_add_fusion.2
  149.4 4.6 %bitcast_dynamic-update-slice_fusion.2 = (bf16[4,2048,512]{2,1,0:T(8,128)(2,1)}, bf16[2048,512]{1,0:T(8,128)(2,1)S(1)}) fusion(bf16[4,2048,512]{2,1,0:T(8,128)(2,1)} %get-tuple-element.553, s32[]{:T(128)} %get-tuple-element.551, bf16[4,2048,512]{2,1,0:T(8,128)(2,1)} %get-tuple-element.570, f32[512]{0:T(512)S(1)} %get-tuple-element.569, ...), kind=kOutput, calls=%fused_computation.17.clone.1 | convolution fusion | flops 544210944 | bytes 7609344 | tf_op jit(solution)/shard_map/while/body/eval_jaxpr/dot_general | solution.py:87
  153.9 2.1 convolution_add_fusion.2
  156.0 4.6 %bitcast_dynamic-update-slice_fusion.2 = (bf16[4,2048,512]{2,1,0:T(8,128)(2,1)}, bf16[2048,512]{1,0:T(8,128)(2,1)S(1)}) fusion(bf16[4,2048,512]{2,1,0:T(8,128)(2,1)} %get-tuple-element.553, s32[]{:T(128)} %get-tuple-element.551, bf16[4,2048,512]{2,1,0:T(8,128)(2,1)} %get-tuple-element.570, f32[512]{0:T(512)S(1)} %get-tuple-element.569, ...), kind=kOutput, calls=%fused_computation.17.clone.1 | convolution fusion | flops 544210944 | bytes 7609344 | tf_op jit(solution)/shard_map/while/body/eval_jaxpr/dot_general | solution.py:87
  160.6 2.1 convolution_add_fusion.2
  162.7 0.8 copy-done.1
  163.6 9.0 %fusion.33 = f32[8192,256]{1,0:T(8,128)} fusion(bf16[8192,512]{1,0:T(8,128)(2,1)} %bitcast.59, bf16[512,256]{1,0:T(8,128)(2,1)S(1)} %get-tuple-element.584), kind=kOutput, calls=%fused_computation.71 | convolution fusion | flops 2147483648 | bytes 17039360 | tf_op jit(solution)/shard_map/dot_general | solution.py:131
  172.5 16.0 %reduce-scatter.3.cloned.1.call-done = f32[128,256]{1,0:T(8,128)} async-done(((f32[512,256]{1,0:T(8,128)}), f32[128,256]{1,0:T(8,128)}) %reduce-scatter.3.cloned.1.call-update) | async-done | bytes 131088 | tf_op jit(solution)/shard_map/reduce_scatter | solution.py:128
  188.5 1.6 broadcast_multiply_fusion.1
  190.1 150.1 %reduce-scatter.5.cloned.1.call-done = f32[128,256]{1,0:T(8,128)} async-done(((f32[8192,256]{1,0:T(8,128)}), f32[128,256]{1,0:T(8,128)}) %reduce-scatter.5.cloned.1.call-update) | async-done | bytes 131088 | tf_op jit(solution)/shard_map/reduce_scatter | solution.py:130
  340.1 1.6 broadcast_multiply_fusion
  (39 shorter events, 3.6 us)
Async XLA Ops:
  7.2 12.9 %copy-start = (s32[32768]{0:T(1024)S(1)}, s32[32768]{0:T(1024)}, u32[]{:S(2)}) copy-start(s32[32768]{0:T(1024)} %param.16) | copy-start | bytes 393220
  7.2 86.9 %all-gather.6.cloned.1.call-start = ((), (), s32[]{:S(2)}) async-start(), calls=%async_computation.2 | async-start | bytes 4259840 | tf_op jit(solution)/shard_map/all_gather | solution.py:68
  7.9 180.6 %reduce-scatter.3.cloned.1.call-start = ((), (), s32[]{:S(2)}) async-start(), calls=%async_computation.3 | async-start | bytes 655360 | tf_op jit(solution)/shard_map/reduce_scatter | solution.py:128
  94.1 41.9 %copy-start.2 = (f32[512]{0:T(512)S(1)}, f32[512]{0:T(512)}, u32[]{:S(2)}) copy-start(f32[512]{0:T(512)} %param.17) | copy-start | bytes 6148
  162.7 0.8 copy-start.1
  163.5 176.6 %reduce-scatter.5.cloned.1.call-start = ((), (), s32[]{:S(2)}) async-start(), calls=%async_computation.4 | async-start | bytes 8519680 | tf_op jit(solution)/shard_map/reduce_scatter | solution.py:130
Sparse Core Ops, SparseCore 0:
  10.8 83.2 all-gather.5
  163.6 24.8 reduce-scatter.2
  192.7 147.3 reduce-scatter.4
where the time goes:
time: 353 us; the launch traced here: 348 us
  waiting for transfers between devices  234 us (66%)
  matrix products  50.7 us (14%)
  blocking collectives  34 us (10%)
  other arithmetic  14.1 us (4%)
  between operations  13.9 us (4%)
    reduce_scatter x1, waiting for transfers between devices, shards(): lax.psum_scatter(jnp.dot(grad_table, query_rows, preferred_element_type=j...  150 us
    all_gather x1, waiting for transfers between devices, shards(): cand_rows = lax.all_gather(candidates, 'row', axis=0, tiled=True)  66.8 us
    dot_general x8, matrix products, scores_of(): lax.dot_general(cand_block, query_rows, (((1,), (1,)), ((), ())), preferr...  26.3 us
    all_gather x2, blocking collectives, joined(): gathered = jax.tree.map(lambda a: lax.all_gather(a, axis), part)  16.5 us
    reduce_scatter x1, waiting for transfers between devices, shards(): lax.psum_scatter(query_term, 'col', scatter_dimension=0, tiled=True) * scale  16 us
    all_gather x1, blocking collectives, shards(): query_rows = lax.all_gather(queries, 'col', axis=0, tiled=True)  11.2 us
    dot_general x1, matrix products, shards(): jnp.dot(grad_table, query_rows, preferred_element_type=jnp.float32)  8.95 us
    dot_general x4, matrix products, grad_block(): lax.dot_general(grads, inputs[0], (((0,), (0,)), ((), ())), preferred_ele...  8.28 us
  transfers between devices with their start and end apart: 3, of which 3 were waited for; matrix products, arithmetic and copies ran while one was open for 5% of the time, Pallas kernels for 0%

commit v1 on v0

v1 whole, which is shorter than its diff:
```python
import math

import jax
import jax.numpy as jnp
from jax import lax
from jax.experimental import pallas as pl
from jax.experimental.pallas import tpu as pltpu
from jax.sharding import PartitionSpec as P

MESH = pl.DeviceIdType.MESH
F32 = jnp.float32
BF16 = jnp.bfloat16
ROWS = 128
D = 256
NX, NY, NZ = 4, 4, 8
TILE = 2048
SLOTS = 16
CLASSES = 8
GROUP = 512
GROUPS = TILE // GROUP
NB = 256
LOG2E = math.log2(math.e)
NT = (((1,), (1,)), ((), ()))
TN = (((0,), (0,)), ((), ()))

OFFSETS = [(0, 0), (1, 0), (3, 0), (2, 0), (0, 1), (0, 3), (0, 2)]
OFFSETS += [(a, b) for a in (1, 3, 2) for b in (1, 3, 2)]
PLACE = {o: i for i, o in enumerate(OFFSETS)}


def split2(value):
    high = value.astype(BF16)
    return high, (value - high.astype(F32)).astype(BF16)


def as_row(value):
    return jnp.concatenate([value[s : s + 1, :] for s in range(SLOTS)], axis=1)


def kernel(
    q_own, c_own, mask_ref, rc_ref, cc_ref, cot_ref, dq_out, dc_out,
    qg, cg, qt, e, m_ref, l_ref, pt, pc, ot, post, st_own, st_sib, st_all, aqt,
    dqf, dcf, zs_sib, zr_sib, zp, zs1, zr1, zs2, zr2, xs1, xr1, xs2, xr2,
    q_ss, q_rs, qf_ss, qf_rs, c_ss, c_rs, t_ss, t_rs, zb_ss, zb_rs,
    z1_ss, z1_rs, z2_ss, z2_rs, x1_ss, x1_rs, x2_ss, x2_rs,
):
    scale = 1.0 / math.sqrt(D)
    kk = LOG2E * scale
    x = lax.axis_index("col")
    row = lax.axis_index("row")
    core = row % 2
    z = (row // 2) % NZ
    y = row // (2 * NZ)
    par = (x + y) % 2
    zpar = z % 2
    zsig = 1 - 2 * zpar

    def dev(dx, dy, dz, dcore):
        ny, nz, nc = (y + dy) % NY, (z + dz) % NZ, (core + dcore) % 2
        return ((ny * NZ + nz) * 2 + nc, (x + dx) % NX)

    sibling = dev(0, 0, 0, 1)
    pending = []

    def send(src, dst, ssem, rsem, to):
        copy = pltpu.make_async_remote_copy(
            src_ref=src, dst_ref=dst, send_sem=ssem, recv_sem=rsem, device_id=to, device_id_type=MESH
        )
        copy.start()
        pending.append(copy)
        return copy

    def arrived(dst, ssem, rsem):
        pltpu.make_async_remote_copy(
            src_ref=dst, dst_ref=dst, send_sem=ssem, recv_sem=rsem, device_id=sibling, device_id_type=MESH
        ).wait_recv()

    barrier = pltpu.get_barrier_semaphore()
    peers = [sibling]
    peers += [dev(d, 0, 0, 0) for d in (1, 2, 3)]
    peers += [dev(0, d, 0, 0) for d in (1, 2, 3)]
    peers += [dev(0, 0, d, 0) for d in (1, 2, 6, 7)]
    for peer in peers:
        pl.semaphore_signal(barrier, inc=1, device_id=peer, device_id_type=MESH)
    pl.semaphore_wait(barrier, len(peers))

    own_slot = 2 * z + core
    z_hops = (2, -2, 1, -1)
    for i, hop in enumerate(z_hops):
        send(q_own, qg.at[own_slot], q_ss.at[i], q_rs.at[i], dev(0, 0, hop, 0))
    for o in OFFSETS[1:7]:
        back = ((-o[0]) % NX, (-o[1]) % NY)
        send(c_own, cg.at[PLACE[back]], c_ss.at[PLACE[back]], c_rs.at[PLACE[back]], dev(o[0], o[1], 0, 0))
    send(q_own, qg.at[own_slot], qf_ss.at[7], qf_rs.at[7], sibling)
    qg[own_slot] = q_own[...]
    cg[0] = c_own[...]

    lane256 = lax.broadcasted_iota(jnp.int32, (SLOTS, NB), 1)
    slot256 = lax.broadcasted_iota(jnp.int32, (SLOTS, NB), 0)
    sel_q = jnp.where(lane256 == (y * SLOTS + slot256) * NX + x, 1.0, 0.0).astype(BF16)
    c_block = jnp.zeros((SLOTS, NB), jnp.int32)
    for b, (dx, dy) in enumerate(OFFSETS):
        block = ((((y + dy) % NY) * NZ + z) * 2 + core) * NX + (x + dx) % NX
        c_block = jnp.where(slot256 == b, block, c_block)
    sel_c = jnp.where(lane256 == c_block, 1.0, 0.0).astype(BF16)
    mask = mask_ref[...].astype(F32).astype(BF16)
    rc_all = rc_ref[...].astype(F32).astype(BF16)
    cc_all = cc_ref[...].astype(F32)
    m_sel = jnp.dot(sel_q, mask, preferred_element_type=F32).astype(BF16)
    rc = jnp.dot(sel_q, rc_all, preferred_element_type=F32)
    cc = jnp.dot(sel_c, cc_all.astype(BF16), preferred_element_type=F32)
    lane128 = lax.broadcasted_iota(jnp.int32, (ROWS, ROWS), 1)
    hist = jnp.zeros((NB, ROWS), F32)
    for k in range(CLASSES):
        column = jnp.where(lane128 == k, 1.0, 0.0).astype(BF16)
        same = jnp.where(cc_all == float(k), 1.0, 0.0).astype(BF16)
        hist = hist + jnp.dot(same, column, preferred_element_type=F32)
    per_class = jnp.dot(m_sel, hist.astype(BF16), preferred_element_type=F32)
    count = jnp.zeros((SLOTS, ROWS), F32)
    for k in range(CLASSES):
        count = jnp.where(rc == float(k), per_class[:, k : k + 1], count)
    denom = jnp.maximum(count, 1.0)
    class_of = (lax.broadcasted_iota(jnp.int32, (ROWS, ROWS), 0) % CLASSES).astype(F32)
    slot_of = lax.broadcasted_iota(jnp.int32, (ROWS, ROWS), 0) // CLASSES

    def repeated(value):
        return jnp.broadcast_to(value[:, None, :], (SLOTS, CLASSES, NB)).reshape(ROWS, NB)

    sel_c_rows = repeated(sel_c.astype(F32)).astype(BF16)
    m_sel_rows = repeated(m_sel.astype(F32)).astype(BF16)
    hit_q = lax.dot_general(sel_c_rows, m_sel, NT, preferred_element_type=F32)
    hit_c = lax.dot_general(m_sel_rows, sel_c, NT, preferred_element_type=F32)
    for s in range(SLOTS):
        lanes = slice(s * ROWS, (s + 1) * ROWS)
        picked = jnp.where(rc[s : s + 1, :] == class_of, hit_q[:, s : s + 1], 0.0).astype(BF16)
        pt[0:ROWS, lanes] = picked
        pt[ROWS:NB, lanes] = picked
        picked = jnp.where(cc[s : s + 1, :] == class_of, hit_c[:, s : s + 1], 0.0).T.astype(BF16)
        pc[lanes, 0:ROWS] = picked
        pc[lanes, ROWS:NB] = picked

    def c_slot(even, odd):
        return even + par * (odd - even)

    turn = [
        (c_slot(4, 1), 1 - par, par, [((d, 0), (0, d)) for d in (1, 3, 2)], ((0, 1), (1, 0))),
        (c_slot(5, 2), 1 - par, par, [((d, 0), (0, d)) for d in (1, 3, 2)], ((0, 3), (3, 0))),
        (c_slot(3, 6), par, 1 - par, [((0, d), (d, 0)) for d in (1, 3, 2)], ((2, 0), (0, 2))),
    ]
    sent = 0
    for slot, fx, fy, hops, origin in turn:
        arrived(cg.at[slot], c_ss.at[slot], c_rs.at[slot])
        for even, odd in hops:
            d = max(even)
            there = [
                PLACE[((o[0] - h[0]) % NX, (o[1] - h[1]) % NY)] for o, h in zip(origin, (even, odd))
            ]
            there = c_slot(*there)
            send(cg.at[slot], cg.at[there], c_ss.at[7 + sent], c_rs.at[there], dev(fx * d, fy * d, 0, 0))
            sent += 1

    def q_slot(dz):
        return 2 * ((z + dz) % NZ) + core

    def pass_on(i, dz):
        slot = q_slot(dz)
        send(qg.at[slot], qg.at[slot], qf_ss.at[i], qf_rs.at[i], sibling)

    for i in (0, 1):
        slot = q_slot(-z_hops[i])
        arrived(qg.at[slot], q_ss.at[i], q_rs.at[i])
    far = q_slot(-2 * zsig)
    send(qg.at[far], qg.at[far], q_ss.at[4], q_rs.at[4], dev(0, 0, 2 * zsig, 0))
    slot = q_slot(-2)
    send(qg.at[slot], qg.at[slot], q_ss.at[5], q_rs.at[5], dev(0, 0, 1, 0))
    slot = q_slot(2)
    send(qg.at[slot], qg.at[slot], q_ss.at[6], q_rs.at[6], dev(0, 0, -1, 0))
    pass_on(0, -2)
    pass_on(1, 2)
    for i in (2, 3):
        slot = q_slot(-z_hops[i])
        arrived(qg.at[slot], q_ss.at[i], q_rs.at[i])
        pass_on(i, -z_hops[i])
    for i, dz in ((4, 4), (5, -3), (6, 3)):
        slot = q_slot(dz)
        arrived(qg.at[slot], q_ss.at[i], q_rs.at[i])
        pass_on(i, dz)
    for i, dz in ((7, 0), (0, -2), (1, 2), (2, -1), (3, 1), (4, 4), (5, -3), (6, 3)):
        slot = 2 * ((z + dz) % NZ) + 1 - core
        arrived(qg.at[slot], qf_ss.at[i], qf_rs.at[i])
    for slot in (c_slot(1, 4), c_slot(2, 5), c_slot(6, 3)):
        arrived(cg.at[slot], c_ss.at[slot], c_rs.at[slot])

    q_all = qg[...].reshape(TILE, D)
    for g in range(GROUPS):
        first = g * GROUP // ROWS
        for slot in range(max(first, 7), first + GROUP // ROWS):
            arrived(cg.at[slot], c_ss.at[slot], c_rs.at[slot])
        rows = slice(g * GROUP, (g + 1) * GROUP)
        c_rows = cg[first : first + GROUP // ROWS].reshape(GROUP, D)
        scores = lax.dot_general(c_rows, q_all, NT, preferred_element_type=F32)
        top = jnp.max(scores, axis=0, keepdims=True)
        grown = jnp.exp2((scores - top) * kk)
        m_ref[g : g + 1, :] = top
        l_ref[g : g + 1, :] = jnp.sum(grown, axis=0, keepdims=True)
        e[rows, :] = grown.astype(BF16)
    m_groups = m_ref[0:GROUPS, :]
    m_tile = jnp.max(m_groups, axis=0, keepdims=True)
    shrink = jnp.exp2((m_groups - m_tile) * kk)
    l_tile = jnp.sum(l_ref[0:GROUPS, :] * shrink, axis=0, keepdims=True)

    for s in range(SLOTS):
        lanes = slice(s * ROWS, (s + 1) * ROWS)
        st_own[s : s + 1, :] = m_tile[:, lanes]
        st_own[SLOTS + s : SLOTS + s + 1, :] = l_tile[:, lanes]
    st_own[32:40, :] = jnp.broadcast_to(cot_ref[pl.ds(x, 1), :], (8, ROWS))
    send(st_own, st_sib, t_ss.at[0], t_rs.at[0], sibling)
    for s in range(SLOTS):
        lanes = slice(s * ROWS, (s + 1) * ROWS)
        qt[:, lanes] = qg[s].T
    arrived(st_sib, t_ss.at[0], t_rs.at[0])
    m_a, m_b = st_own[0:SLOTS, :], st_sib[0:SLOTS, :]
    m_pair = jnp.maximum(m_a, m_b)
    l_pair = st_own[SLOTS:32, :] * jnp.exp2((m_a - m_pair) * kk)
    l_pair = l_pair + st_sib[SLOTS:32, :] * jnp.exp2((m_b - m_pair) * kk)
    cot_a, cot_b = st_own[32:40, :], st_sib[32:40, :]
    here = lax.broadcasted_iota(jnp.int32, (8, ROWS), 0) == core
    st_all[z, 0:SLOTS, :] = m_pair
    st_all[z, SLOTS:32, :] = l_pair
    st_all[z, 32:40, :] = jnp.where(here, cot_a, cot_b)
    for d in range(1, NZ):
        send(st_all.at[z], st_all.at[z], t_ss.at[d], t_rs.at[d], dev(0, 0, d, 0))

    for g in range(GROUPS):
        first = g * GROUP // ROWS
        rows = slice(g * GROUP, (g + 1) * GROUP)
        c_rows = cg[first : first + GROUP // ROWS].reshape(GROUP, D)
        part = lax.dot_general(c_rows, e[rows, :], TN, preferred_element_type=F32) * shrink[g : g + 1, :]
        if g == 0:
            ot[...] = part
        else:
            ot[...] += part
    own_class = [
        jnp.where((cc[b : b + 1, :] == class_of) & (slot_of == b), 1.0, 0.0).astype(BF16) for b in range(SLOTS)
    ]
    sums = jnp.dot(
        jnp.concatenate(own_class, axis=1), cg[...].reshape(TILE, D), preferred_element_type=F32
    )
    sums = jnp.concatenate(split2(sums), axis=0)
    post[...] = lax.dot_general(sums, pt[...], TN, preferred_element_type=F32)

    for d in range(1, NZ):
        slot = (z - d + NZ) % NZ
        arrived(st_all.at[slot], t_ss.at[d], t_rs.at[d])
    m_all = st_all[0, 0:SLOTS, :]
    for s in range(1, NZ):
        m_all = jnp.maximum(m_all, st_all[s, 0:SLOTS, :])
    l_all = jnp.zeros((SLOTS, ROWS), F32)
    for s in range(NZ):
        l_all = l_all + st_all[s, SLOTS:32, :] * jnp.exp2((st_all[s, 0:SLOTS, :] - m_all) * kk)
    cot = jnp.concatenate([st_all[s, 32:34, :] for s in range(NZ)], axis=0)
    coef_pos = cot / denom
    soft = cot * count / denom / l_all
    soft_row, top_row, pos_row = as_row(soft), as_row(m_all), as_row(coef_pos)
    a_groups = soft_row * jnp.exp2((m_groups - top_row) * kk)
    a_tile = soft_row * jnp.exp2((m_tile - top_row) * kk)

    def dq_tile(slot):
        lanes = pl.ds(pl.multiple_of(slot * ROWS, ROWS), ROWS)
        return lanes

    dq_all = ot[...] * a_tile - post[...] * pos_row
    for s in range(SLOTS):
        dqf[s] = dq_all[:, s * ROWS : (s + 1) * ROWS]
    for s in range(NZ):
        zs_sib[s] = dqf[2 * s + 1 - core].astype(BF16)
    send(zs_sib, zr_sib, zb_ss.at[0], zb_rs.at[0], sibling)

    weights = [
        jnp.where((rc[s : s + 1, :] == class_of) & (slot_of == s), -coef_pos[s : s + 1, :], 0.0)
        for s in range(SLOTS)
    ]
    weights = jnp.concatenate(split2(jnp.concatenate(weights, axis=1)), axis=0)
    sums_q = jnp.dot(weights, q_all, preferred_element_type=F32)
    sums_q = sums_q[0:ROWS, :] + sums_q[ROWS:NB, :]
    sums_q = jnp.concatenate(split2(sums_q), axis=0)

    def dc_group(g):
        first = g * GROUP // ROWS
        rows = slice(g * GROUP, (g + 1) * GROUP)
        aqt[...] = (qt[...].astype(F32) * a_groups[g : g + 1, :]).astype(BF16)
        part = lax.dot_general(e[rows, :], aqt[...], NT, preferred_element_type=F32)
        part = part + jnp.dot(pc[rows, :], sums_q, preferred_element_type=F32)
        dcf[first : first + GROUP // ROWS] = part.reshape(GROUP // ROWS, ROWS, D)

    hub = {2: 0, 1: 1, 3: 2}

    def dc_send(slot):
        a, b = OFFSETS[slot]
        i = slot - 7
        odd = (par + a + b) % 2
        xs1[i] = dcf[slot].astype(BF16)
        even_to = hub[a] * 3 + (-b) % NY - 1
        odd_to = hub[b] * 3 + (-a) % NX - 1
        there = even_to + odd * (odd_to - even_to)
        send(xs1.at[i], xr1.at[there], x1_ss.at[i], x1_rs.at[there], dev(odd * a, (1 - odd) * b, 0, 0))

    dc_group(3)
    for slot in (12, 13, 14, 15):
        dc_send(slot)

    arrived(zr_sib, zb_ss.at[0], zb_rs.at[0])
    for s in range(NZ):
        zp[s] = dqf[2 * s + core] + zr_sib[s].astype(F32)
    for i, (target, hop) in enumerate(((-3, -1), (3, 1), (4, -2 * zsig))):
        zs1[i] = zp[(z + target + NZ) % NZ].astype(BF16)
        send(zs1.at[i], zr1.at[i], z1_ss.at[i], z1_rs.at[i], dev(0, 0, hop, 0))
    for i, target in ((2, -1), (3, 1)):
        zs2[i] = zp[(z + target + NZ) % NZ].astype(BF16)
        send(zs2.at[i], zr2.at[i], z2_ss.at[i], z2_rs.at[i], dev(0, 0, target, 0))

    dc_group(2)
    for slot in (8, 9, 10, 11):
        dc_send(slot)
    dc_group(1)
    dc_send(7)
    dc_group(0)
    for i, (slot, there, even, odd) in enumerate(
        (
            (c_slot(6, 3), c_slot(6, 3), (0, 2), (2, 0)),
            (c_slot(1, 4), c_slot(2, 5), (1, 0), (0, 1)),
            (c_slot(2, 5), c_slot(1, 4), (3, 0), (0, 3)),
        )
    ):
        xs2[i] = dcf[slot].astype(BF16)
        to = dev(even[0] + par * (odd[0] - even[0]), even[1] + par * (odd[1] - even[1]), 0, 0)
        send(xs2.at[i], xr2.at[there - 1], x2_ss.at[i], x2_rs.at[there - 1], to)

    for i in range(3):
        arrived(zr1.at[i], z1_ss.at[i], z1_rs.at[i])
    far = zr1[2].astype(F32)
    down = zp[(z + NZ - 2) % NZ] + zr1[0].astype(F32) + jnp.where(zpar == 0, far, 0.0)
    up = zp[(z + 2) % NZ] + zr1[1].astype(F32) + jnp.where(zpar == 1, far, 0.0)
    zs2[0] = down.astype(BF16)
    zs2[1] = up.astype(BF16)
    send(zs2.at[0], zr2.at[0], z2_ss.at[0], z2_rs.at[0], dev(0, 0, -2, 0))
    send(zs2.at[1], zr2.at[1], z2_ss.at[1], z2_rs.at[1], dev(0, 0, 2, 0))

    for j, (slot, there, even, odd) in enumerate(
        (
            (c_slot(3, 6), c_slot(3, 6), (2, 0), (0, 2)),
            (c_slot(4, 1), c_slot(5, 2), (0, 1), (1, 0)),
            (c_slot(5, 2), c_slot(4, 1), (0, 3), (3, 0)),
        )
    ):
        total = dcf[slot]
        for d in range(3):
            arrived(xr1.at[3 * j + d], x1_ss.at[3 * j + d], x1_rs.at[3 * j + d])
            total = total + xr1[3 * j + d].astype(F32)
        xs2[3 + j] = total.astype(BF16)
        to = dev(even[0] + par * (odd[0] - even[0]), even[1] + par * (odd[1] - even[1]), 0, 0)
        send(xs2.at[3 + j], xr2.at[there - 1], x2_ss.at[3 + j], x2_rs.at[there - 1], to)

    total = zp[z]
    for i in (2, 3, 0, 1):
        arrived(zr2.at[i], z2_ss.at[i], z2_rs.at[i])
        total = total + zr2[i].astype(F32)
    dq_out[...] = total.T * scale
    total = dcf[0]
    for i in range(6):
        arrived(xr2.at[i], x2_ss.at[i], x2_rs.at[i])
        total = total + xr2[i].astype(F32)
    dc_out[...] = total * scale
    for copy in pending:
        copy.wait_send()


def shards(queries, candidates, block_mask, row_class, col_class, cotangent):
    dma = pltpu.SemaphoreType.DMA
    vmem = pltpu.VMEM
    block = (D, ROWS)
    scratch = [
        vmem((SLOTS, ROWS, D), BF16),
        vmem((SLOTS, ROWS, D), BF16),
        vmem((D, TILE), BF16),
        vmem((TILE, TILE), BF16),
        vmem((8, TILE), F32),
        vmem((8, TILE), F32),
        vmem((NB, TILE), BF16),
        vmem((TILE, NB), BF16),
        vmem((D, TILE), F32),
        vmem((D, TILE), F32),
        vmem((40, ROWS), F32),
        vmem((40, ROWS), F32),
        vmem((NZ, 40, ROWS), F32),
        vmem((D, TILE), BF16),
        vmem((SLOTS,) + block, F32),
        vmem((SLOTS, ROWS, D), F32),
        vmem((NZ,) + block, BF16),
        vmem((NZ,) + block, BF16),
        vmem((NZ,) + block, F32),
        vmem((3,) + block, BF16),
        vmem((3,) + block, BF16),
        vmem((4,) + block, BF16),
        vmem((4,) + block, BF16),
        vmem((9, ROWS, D), BF16),
        vmem((9, ROWS, D), BF16),
        vmem((6, ROWS, D), BF16),
        vmem((6, ROWS, D), BF16),
        dma((7,)), dma((7,)), dma((8,)), dma((8,)), dma((16,)), dma((16,)), dma((8,)), dma((8,)),
        dma((1,)), dma((1,)), dma((3,)), dma((3,)), dma((4,)), dma((4,)),
        dma((9,)), dma((9,)), dma((6,)), dma((6,)),
    ]
    out = jax.ShapeDtypeStruct((ROWS, D), F32)
    return pl.pallas_call(
        kernel,
        out_shape=(out, out),
        in_specs=[pl.BlockSpec(memory_space=vmem)] * 6,
        out_specs=(pl.BlockSpec(memory_space=vmem), pl.BlockSpec(memory_space=vmem)),
        scratch_shapes=scratch,
        compiler_params=pltpu.CompilerParams(
            collective_id=0, has_side_effects=True, vmem_limit_bytes=56 * 2**20
        ),
    )(
        queries,
        candidates,
        block_mask,
        row_class.reshape(NB, ROWS),
        col_class.reshape(NB, ROWS),
        cotangent.reshape(NX, ROWS),
    )


def solution(mesh):
    in_specs = (P(("row", "col"), None), P(("row", "col"), None), P(), P(), P(), P("row"))
    out_specs = (P(("row", "col"), None), P(("row", "col"), None))
    return jax.shard_map(shards, mesh=mesh, in_specs=in_specs, out_specs=out_specs, check_vma=False)
```

time: 353 us -> 55.2 us (0.16); the launches traced: 348 us -> 55.1 us
  waiting for transfers between devices: 234 us -> 0 us
  Pallas kernels: 0 us -> 52.2 us
  matrix products: 50.7 us -> 0 us
  blocking collectives: 34 us -> 0 us
  other arithmetic: 14.1 us -> 0 us
  between operations: 13.9 us -> 0.65 us
    reduce_scatter x2 -> x0, waiting for transfers between devices: 166 us -> none  [the longest x1 150 us: shards(): lax.psum_scatter(jnp.dot(grad_table, query_rows, preferred_element_type=j...]
    all_gather x1 -> x0, waiting for transfers between devices: 66.8 us -> none  [shards(): cand_rows = lax.all_gather(candidates, 'row', axis=0, tiled=True)]
    pallas_call x0 -> x1, Pallas kernels: none -> 52.2 us  [shards(): pl.pallas_call(kernel, out_shape=(out, out), in_specs=[pl.BlockSpec(memor...]
    dot_general x14 -> x0, matrix products: 50.7 us -> none  [the longest x8 26.3 us: scores_of(): lax.dot_general(cand_block, query_rows, (((1,), (1,)), ((), ())), preferr...]
    all_gather x3 -> x0, blocking collectives: 27.7 us -> none  [the longest x2 16.5 us: joined(): gathered = jax.tree.map(lambda a: lax.all_gather(a, axis), part)]
    reduce_sum x8 -> x0, other arithmetic: 10.8 us -> none  [the longest x4 7.75 us: gather_stats(): block_count = jnp.sum(inputs[1].astype(jnp.float32), axis=0)]
    psum x1 -> x0, blocking collectives: 6.36 us -> none  [shards(): row_count = lax.psum(row_count, 'col')]
  transfers between devices with their start and end apart: 3 -> 0, of which waited for: 3 -> 0; matrix products, arithmetic and copies ran while one was open for 5% -> 0% of each run, Pallas kernels for 0% -> 0%
where the time goes in v1:
time: 55.2 us; the launch traced here: 55.1 us
  Pallas kernels  52.2 us (95%)
  local copies, waits for them, and re-layouts  2.26 us (4%)
  between operations  0.65 us (1%)
    pallas_call x1, Pallas kernels, shards(): pl.pallas_call(kernel, out_shape=(out, out), in_specs=[pl.BlockSpec(memor...  52.2 us
    unnamed x4, local copies, waits for them, and re-layouts  2.26 us

profile of v1, /device:TPU:1, one launch (start us, length us, event | category | flops | bytes accessed | tf_op | source)
XLA Modules:
  0.0 55.1 jit_solution(1544363430676915154)
XLA Ops:
  0.6 52.2 %shard_map.77 = (f32[128,256]{1,0:T(8,128)}, f32[128,256]{1,0:T(8,128)}) custom-call(bf16[128,256]{1,0:T(8,128)(2,1)} %q_own.1, bf16[128,256]{1,0:T(8,128)(2,1)} %c_own.1, s32[256,256]{1,0:T(8,128)} %mask_ref.1, s32[256,128]{1,0:T(8,128)} %bitcast.3, s32[256,128]{1,0:T(8,128)} %bitcast.4, f32[4,128]{1,0:T(4,128)} %bitcast.5), custom_call_target="tpu_custom_call" | custom-call | tf_op jit(solution)/shard_map/pallas_call | solution.py:415
  52.8 0.0 copy-start
  52.8 1.6 %copy.10 = f32[128,256]{1,0:T(8,128)} copy(f32[128,256]{1,0:T(8,128)} %get-tuple-element.4) | data formatting | bytes 262144
  54.4 0.0 copy-done
  54.4 0.7 %copy.11 = f32[128,256]{1,0:T(8,128)} copy(f32[128,256]{1,0:T(8,128)S(1)} %copy-done) | data formatting | bytes 262144
Async XLA Ops:
  52.8 1.6 %copy-start = (f32[128,256]{1,0:T(8,128)S(1)}, f32[128,256]{1,0:T(8,128)}, u32[]{:S(2)}) copy-start(f32[128,256]{1,0:T(8,128)} %get-tuple-element.5) | copy-start | bytes 393220

commit v2 on v1

v2 whole, which is shorter than its diff:
```python
import math

import jax
import jax.numpy as jnp
from jax import lax
from jax.experimental import pallas as pl
from jax.experimental.pallas import tpu as pltpu
from jax.sharding import PartitionSpec as P

MESH = pl.DeviceIdType.MESH
F32 = jnp.float32
BF16 = jnp.bfloat16
ROWS = 128
D = 256
NX, NY, NZ = 4, 4, 8
TILE = 2048
SLOTS = 16
CLASSES = 8
NB = 256
LOG2E = math.log2(math.e)
NT = (((1,), (1,)), ((), ()))
TN = (((0,), (0,)), ((), ()))

OFFSETS = [(0, 0), (1, 0), (3, 0), (2, 0), (0, 1), (0, 3), (0, 2)]
OFFSETS += [(1, 1), (1, 3), (3, 1), (3, 3), (1, 2), (3, 2), (2, 1), (2, 3), (2, 2)]
PLACE = {o: i for i, o in enumerate(OFFSETS)}
GROUPS = ((0, 7), (7, 10), (10, 13), (13, 16))
Q_OFFSETS = [(0, 0), (-2, 0), (2, 0), (-1, 0), (0, 1), (-2, 1), (2, 1), (-1, 1)]
Q_OFFSETS += [(1, 0), (4, 0), (-3, 0), (3, 0), (1, 1), (4, 1), (-3, 1), (3, 1)]
Q_PLACE = {o: i for i, o in enumerate(Q_OFFSETS)}
OWN_CORE = (0, 1, 2, 3, 8, 9, 10, 11)


def split2(value):
    high = value.astype(BF16)
    return high, (value - high.astype(F32)).astype(BF16)


def as_row(rows):
    return jnp.concatenate(rows, axis=1)


def lanes_of(slot):
    return slice(slot * ROWS, (slot + 1) * ROWS)


def kernel(
    q_own, c_own, mask_hbm, rc_hbm, cc_hbm, cot_hbm, dq_out, dc_out,
    mask_ref, rc_ref, cc_ref, cot_ref, aux,
    qg, cg, qt, e, m_ref, l_ref, pt, pc, ot, post, st_own, st_sib, st_all, st_end, aqt,
    dcf, zs_sib, zr_sib, zp, zs1, zr1, zs2, zr2, xs1, xr1, xs2, xr2,
    in_s, q_ss, q_rs, qf_ss, qf_rs, a_ss, a_rs, af_ss, af_rs, c_ss, c_rs, t_ss, t_rs, zb_ss, zb_rs,
    z1_ss, z1_rs, z2_ss, z2_rs, x1_ss, x1_rs, x2_ss, x2_rs,
):
    kk = LOG2E / math.sqrt(D)
    x = lax.axis_index("col")
    row = lax.axis_index("row")
    core = row % 2
    z = (row // 2) % NZ
    y = row // (2 * NZ)
    par = (x + y) % 2
    zpar = z % 2
    zsig = 1 - 2 * zpar

    def dev(dx, dy, dz, dcore):
        ny, nz, nc = (y + dy) % NY, (z + dz) % NZ, (core + dcore) % 2
        return ((ny * NZ + nz) * 2 + nc, (x + dx) % NX)

    sibling = dev(0, 0, 0, 1)
    pending = []

    def send(src, dst, ssem, rsem, to):
        copy = pltpu.make_async_remote_copy(
            src_ref=src, dst_ref=dst, send_sem=ssem, recv_sem=rsem, device_id=to, device_id_type=MESH
        )
        copy.start()
        pending.append(copy)

    def arrived(dst, ssem, rsem):
        pltpu.make_async_remote_copy(
            src_ref=dst, dst_ref=dst, send_sem=ssem, recv_sem=rsem, device_id=sibling, device_id_type=MESH
        ).wait_recv()

    barrier = pltpu.get_barrier_semaphore()
    peers = [dev(0, 0, d, 0) for d in (2, 6, 1, 7)]
    peers += [dev(d, 0, 0, 0) for d in (2, 1, 3)]
    peers += [dev(0, d, 0, 0) for d in (2, 1, 3)]
    peers += [sibling]
    for peer in peers:
        pl.semaphore_signal(barrier, inc=1, device_id=peer, device_id_type=MESH)
    loads = [
        pltpu.make_async_copy(src, dst, in_s.at[i])
        for i, (src, dst) in enumerate(
            (
                (cot_hbm, cot_ref), (mask_hbm, mask_ref), (rc_hbm, rc_ref), (cc_hbm, cc_ref),
                (q_own, qg.at[0]), (c_own, cg.at[0]),
            )
        )
    ]
    for load in loads:
        load.start()
    pl.semaphore_wait(barrier, len(peers))

    z_hops = (2, -2, 1, -1)
    for i, hop in enumerate(z_hops):
        send(q_own, qg.at[Q_PLACE[-hop, 0]], q_ss.at[i], q_rs.at[i], dev(0, 0, hop, 0))
    for o in OFFSETS[1:7]:
        back = PLACE[(-o[0]) % NX, (-o[1]) % NY]
        send(c_own, cg.at[back], c_ss.at[back], c_rs.at[back], dev(o[0], o[1], 0, 0))
    send(q_own, qg.at[Q_PLACE[0, 1]], qf_ss.at[7], qf_rs.at[7], sibling)
    for load in loads:
        load.wait()
    aux[0] = jnp.broadcast_to(cot_ref[pl.ds(x, 1), :], (8, ROWS))
    for i, hop in enumerate(z_hops):
        send(aux.at[0], aux.at[Q_PLACE[-hop, 0]], a_ss.at[i], a_rs.at[i], dev(0, 0, hop, 0))
    send(aux.at[0], aux.at[Q_PLACE[0, 1]], af_ss.at[7], af_rs.at[7], sibling)

    lane256 = lax.broadcasted_iota(jnp.int32, (SLOTS, NB), 1)
    slot256 = lax.broadcasted_iota(jnp.int32, (SLOTS, NB), 0)
    q_block = jnp.zeros((SLOTS, NB), jnp.int32)
    for s, (dz, dc) in enumerate(Q_OFFSETS):
        block = ((y * NZ + (z + dz) % NZ) * 2 + (core + dc) % 2) * NX + x
        q_block = jnp.where(slot256 == s, block, q_block)
    sel_q = jnp.where(lane256 == q_block, 1.0, 0.0).astype(BF16)
    c_block = jnp.zeros((SLOTS, NB), jnp.int32)
    for b, (dx, dy) in enumerate(OFFSETS):
        block = ((((y + dy) % NY) * NZ + z) * 2 + core) * NX + (x + dx) % NX
        c_block = jnp.where(slot256 == b, block, c_block)
    sel_c = jnp.where(lane256 == c_block, 1.0, 0.0).astype(BF16)
    mask = mask_ref[...].astype(F32).astype(BF16)
    rc_all = rc_ref[...].astype(F32).astype(BF16)
    cc_all = cc_ref[...].astype(F32)
    m_sel = jnp.dot(sel_q, mask, preferred_element_type=F32).astype(BF16)
    rc = jnp.dot(sel_q, rc_all, preferred_element_type=F32)
    cc = jnp.dot(sel_c, cc_all.astype(BF16), preferred_element_type=F32)
    lane128 = lax.broadcasted_iota(jnp.int32, (ROWS, ROWS), 1)
    hist = jnp.zeros((NB, ROWS), F32)
    for k in range(CLASSES):
        column = jnp.where(lane128 == k, 1.0, 0.0).astype(BF16)
        same = jnp.where(cc_all == float(k), 1.0, 0.0).astype(BF16)
        hist = hist + jnp.dot(same, column, preferred_element_type=F32)
    per_class = jnp.dot(m_sel, hist.astype(BF16), preferred_element_type=F32)
    count = jnp.zeros((SLOTS, ROWS), F32)
    for k in range(CLASSES):
        count = jnp.where(rc == float(k), per_class[:, k : k + 1], count)
    per_count = 1.0 / jnp.maximum(count, 1.0)
    class_of = (lax.broadcasted_iota(jnp.int32, (ROWS, ROWS), 0) % CLASSES).astype(F32)
    slot_of = lax.broadcasted_iota(jnp.int32, (ROWS, ROWS), 0) // CLASSES

    def repeated(value):
        return jnp.broadcast_to(value[:, None, :], (SLOTS, CLASSES, NB)).reshape(ROWS, NB)

    sel_c_rows = repeated(sel_c.astype(F32)).astype(BF16)
    m_sel_rows = repeated(m_sel.astype(F32)).astype(BF16)
    hit_q = lax.dot_general(sel_c_rows, m_sel, NT, preferred_element_type=F32)
    hit_c = lax.dot_general(m_sel_rows, sel_c, NT, preferred_element_type=F32)
    for s in range(SLOTS):
        picked = jnp.where(rc[s : s + 1, :] == class_of, hit_q[:, s : s + 1], 0.0).astype(BF16)
        pt[0:ROWS, lanes_of(s)] = picked
        pt[ROWS:NB, lanes_of(s)] = picked
        picked = jnp.where(cc[s : s + 1, :] == class_of, hit_c[:, s : s + 1], 0.0).T.astype(BF16)
        pc[lanes_of(s), 0:ROWS] = picked
        pc[lanes_of(s), ROWS:NB] = picked

    def c_slot(even, odd):
        return even + par * (odd - even)

    turn = [
        (c_slot(4, 1), 1 - par, par, [((d, 0), (0, d)) for d in (1, 3, 2)], ((0, 1), (1, 0))),
        (c_slot(5, 2), 1 - par, par, [((d, 0), (0, d)) for d in (1, 3, 2)], ((0, 3), (3, 0))),
        (c_slot(3, 6), par, 1 - par, [((0, d), (d, 0)) for d in (1, 3, 2)], ((2, 0), (0, 2))),
    ]
    forwards = [0]

    def c_forward(slot, fx, fy, hops, origin):
        arrived(cg.at[slot], c_ss.at[slot], c_rs.at[slot])
        for even, odd in hops:
            d = max(even)
            there = [
                PLACE[((o[0] - h[0]) % NX, (o[1] - h[1]) % NY)] for o, h in zip(origin, (even, odd))
            ]
            there = c_slot(*there)
            i = 7 + forwards[0]
            send(cg.at[slot], cg.at[there], c_ss.at[i], c_rs.at[there], dev(fx * d, fy * d, 0, 0))
            forwards[0] += 1

    def q_arrived(i, dz):
        slot = Q_PLACE[dz, 0]
        arrived(qg.at[slot], q_ss.at[i], q_rs.at[i])

    def q_pass(i, dz):
        here, there = Q_PLACE[dz, 0], Q_PLACE[dz, 1]
        send(qg.at[here], qg.at[there], qf_ss.at[i], qf_rs.at[i], sibling)

    def a_pass(i, dz):
        here, there = Q_PLACE[dz, 0], Q_PLACE[dz, 1]
        arrived(aux.at[here], a_ss.at[i], a_rs.at[i])
        send(aux.at[here], aux.at[there], af_ss.at[i], af_rs.at[i], sibling)

    def onward(ref, ss, rs):
        far = Q_PLACE[-2, 0] + zpar * (Q_PLACE[2, 0] - Q_PLACE[-2, 0])
        send(ref.at[far], ref.at[Q_PLACE[4, 0]], ss.at[4], rs.at[4], dev(0, 0, 2 * zsig, 0))
        send(ref.at[Q_PLACE[-2, 0]], ref.at[Q_PLACE[-3, 0]], ss.at[5], rs.at[5], dev(0, 0, 1, 0))
        send(ref.at[Q_PLACE[2, 0]], ref.at[Q_PLACE[3, 0]], ss.at[6], rs.at[6], dev(0, 0, -1, 0))

    c_forward(*turn[0])
    c_forward(*turn[1])
    q_arrived(0, -2)
    q_arrived(1, 2)
    onward(qg, q_ss, q_rs)
    c_forward(*turn[2])
    q_pass(0, -2)
    q_pass(1, 2)
    q_arrived(2, -1)
    q_pass(2, -1)
    q_arrived(3, 1)
    q_pass(3, 1)
    a_pass(0, -2)
    a_pass(1, 2)
    a_pass(2, -1)
    a_pass(3, 1)
    onward(aux, a_ss, a_rs)
    for slot in (c_slot(1, 4), c_slot(2, 5), c_slot(6, 3)):
        arrived(cg.at[slot], c_ss.at[slot], c_rs.at[slot])

    def wave(g, q_first, q_last):
        first, last = GROUPS[g]
        rows = slice(first * ROWS, last * ROWS)
        lanes = slice(q_first * ROWS, q_last * ROWS)
        c_rows = cg[first:last].reshape((last - first) * ROWS, D)
        q_rows = qg[q_first:q_last].reshape((q_last - q_first) * ROWS, D)
        scores = lax.dot_general(c_rows, q_rows, NT, preferred_element_type=F32)
        top = jnp.max(scores, axis=0, keepdims=True)
        grown = jnp.exp2((scores - top) * kk)
        m_ref[g : g + 1, lanes] = top
        l_ref[g : g + 1, lanes] = jnp.sum(grown, axis=0, keepdims=True)
        e[rows, lanes] = grown.astype(BF16)

    wave(0, 0, 4)
    for i, dz in ((7, 0), (0, -2), (1, 2), (2, -1)):
        slot = Q_PLACE[dz, 1]
        arrived(qg.at[slot], qf_ss.at[i], qf_rs.at[i])
    wave(0, 4, 8)
    for i, dz in ((5, -3), (6, 3), (4, 4)):
        q_arrived(i, dz)
        q_pass(i, dz)
    wave(0, 8, 12)
    for i, dz in ((4, 4), (5, -3), (6, 3)):
        a_pass(i, dz)
    for i, dz in ((3, 1), (5, -3), (6, 3), (4, 4)):
        slot = Q_PLACE[dz, 1]
        arrived(qg.at[slot], qf_ss.at[i], qf_rs.at[i])
    wave(0, 12, 16)
    for g in (1, 2, 3):
        for slot in range(*GROUPS[g]):
            arrived(cg.at[slot], c_ss.at[slot], c_rs.at[slot])
        wave(g, 0, 16)
    m_groups = m_ref[0:4, :]
    m_tile = jnp.max(m_groups, axis=0, keepdims=True)
    l_tile = jnp.sum(l_ref[0:4, :] * jnp.exp2((m_groups - m_tile) * kk), axis=0, keepdims=True)

    places = [2 * ((z + dz) % NZ) + (core + dc) % 2 for dz, dc in Q_OFFSETS]

    def slot_rows(ref, start):
        return as_row([ref[pl.ds(start + place, 1), :] for place in places])

    for s, place in enumerate(places):
        st_own[pl.ds(place, 1), :] = m_tile[:, lanes_of(s)]
        st_own[pl.ds(SLOTS + place, 1), :] = l_tile[:, lanes_of(s)]
    send(st_own, st_sib, t_ss.at[0], t_rs.at[0], sibling)
    for s in range(SLOTS):
        qt[:, lanes_of(s)] = qg[s].T
    arrived(st_sib, t_ss.at[0], t_rs.at[0])
    m_a, m_b = st_own[0:SLOTS, :], st_sib[0:SLOTS, :]
    m_pair = jnp.maximum(m_a, m_b)
    l_pair = st_own[SLOTS:32, :] * jnp.exp2((m_a - m_pair) * kk)
    l_pair = l_pair + st_sib[SLOTS:32, :] * jnp.exp2((m_b - m_pair) * kk)
    st_all[z, 0:SLOTS, :] = m_pair
    st_all[z, SLOTS:32, :] = l_pair
    for d in (4, 3, 5, 2, 6, 1, 7):
        send(st_all.at[z], st_all.at[z], t_ss.at[d], t_rs.at[d], dev(0, 0, d, 0))

    m_pair_row = slot_rows(st_all.at[z], 0)
    shrink = jnp.exp2((m_groups - m_pair_row) * kk)
    own_class = [
        jnp.where((cc[b : b + 1, :] == class_of) & (slot_of == b), 1.0, 0.0).astype(BF16) for b in range(SLOTS)
    ]
    sums = jnp.dot(
        jnp.concatenate(own_class, axis=1), cg[...].reshape(TILE, D), preferred_element_type=F32
    )
    sums = jnp.concatenate(split2(sums), axis=0)

    def c_times_e(first):
        lanes = slice(first * ROWS, (first + 4) * ROWS)
        total = None
        for g, (start, stop) in enumerate(GROUPS):
            c_rows = cg[start:stop].reshape((stop - start) * ROWS, D)
            part = lax.dot_general(
                c_rows, e[start * ROWS : stop * ROWS, lanes], TN, preferred_element_type=F32
            )
            part = part * shrink[g : g + 1, lanes]
            total = part if total is None else total + part
        hits = lax.dot_general(sums, pt[:, lanes], TN, preferred_element_type=F32)
        return total, hits

    for half, first in enumerate((4, 12)):
        total, hits = c_times_e(first)
        for s in range(4):
            zs_sib[half, s, 0:D, :] = total[:, lanes_of(s)].astype(BF16)
            zs_sib[half, s, D : 2 * D, :] = hits[:, lanes_of(s)].astype(BF16)
        send(zs_sib.at[half], zr_sib.at[half], zb_ss.at[half], zb_rs.at[half], sibling)
    for half, first in enumerate((0, 8)):
        total, hits = c_times_e(first)
        for s in range(4):
            ot[4 * half + s] = total[:, lanes_of(s)]
            post[4 * half + s] = hits[:, lanes_of(s)]

    for i, dz in ((7, 0), (0, -2), (1, 2), (2, -1), (3, 1), (4, 4), (5, -3), (6, 3)):
        slot = Q_PLACE[dz, 1]
        arrived(aux.at[slot], af_ss.at[i], af_rs.at[i])
    cot = jnp.concatenate([aux[s, 0:1, :] for s in range(SLOTS)], axis=0)
    coef_pos = cot * per_count
    weights = [
        jnp.where((rc[s : s + 1, :] == class_of) & (slot_of == s), -coef_pos[s : s + 1, :], 0.0)
        for s in range(SLOTS)
    ]
    weights = jnp.concatenate(split2(jnp.concatenate(weights, axis=1)), axis=0)
    sums_q = jnp.dot(weights, qg[...].reshape(TILE, D), preferred_element_type=F32)
    sums_q = sums_q[0:ROWS, :] + sums_q[ROWS:NB, :]
    sums_q = jnp.concatenate(split2(sums_q), axis=0)
    soft_row = as_row([(count * per_count)[s : s + 1, :] for s in range(SLOTS)])
    cot_row = as_row([cot[s : s + 1, :] for s in range(SLOTS)])

    for d in (1, 7, 2, 6, 3, 5, 4):
        slot = (z - d + NZ) % NZ
        arrived(st_all.at[slot], t_ss.at[d], t_rs.at[d])
    m_all = st_all[0, 0:SLOTS, :]
    for s in range(1, NZ):
        m_all = jnp.maximum(m_all, st_all[s, 0:SLOTS, :])
    l_all = jnp.zeros((SLOTS, ROWS), F32)
    for s in range(NZ):
        l_all = l_all + st_all[s, SLOTS:32, :] * jnp.exp2((st_all[s, 0:SLOTS, :] - m_all) * kk)
    st_end[0:SLOTS, :] = m_all
    st_end[SLOTS:32, :] = 1.0 / l_all
    top_row, per_mass = slot_rows(st_end, 0), slot_rows(st_end, SLOTS)
    soft_row = soft_row * per_mass
    a_groups = soft_row * cot_row * jnp.exp2((m_groups - top_row) * kk)
    a_pair = soft_row * jnp.exp2((m_pair_row - top_row) * kk)

    def dc_group(g):
        first, last = GROUPS[g]
        rows = slice(first * ROWS, last * ROWS)
        aqt[g % 2] = (qt[...].astype(F32) * a_groups[g : g + 1, :]).astype(BF16)
        part = lax.dot_general(e[rows, :], aqt[g % 2], NT, preferred_element_type=F32)
        part = part + jnp.dot(pc[rows, :], sums_q, preferred_element_type=F32)
        dcf[first:last] = part.reshape(last - first, ROWS, D)

    hub = {2: 0, 1: 1, 3: 2}

    def dc_send(slot):
        a, b = OFFSETS[slot]
        i = slot - 7
        odd = (par + a + b) % 2
        xs1[i] = dcf[slot].astype(BF16)
        even_to = hub[a] * 3 + (-b) % NY - 1
        odd_to = hub[b] * 3 + (-a) % NX - 1
        there = even_to + odd * (odd_to - even_to)
        send(xs1.at[i], xr1.at[there], x1_ss.at[i], x1_rs.at[there], dev(odd * a, (1 - odd) * b, 0, 0))

    dc_group(3)
    for slot in (15, 13, 14):
        dc_send(slot)

    for half in range(2):
        arrived(zr_sib.at[half], zb_ss.at[half], zb_rs.at[half])
    for i, s in enumerate(OWN_CORE):
        lanes = lanes_of(s)
        half, j = i // 4, i % 4
        soft = ot[i] + zr_sib[half, j, 0:D, :].astype(F32)
        hits = post[i] + zr_sib[half, j, D : 2 * D, :].astype(F32)
        zp[i] = soft * a_pair[:, lanes] - hits * per_count[s : s + 1, :]

    def z_part(dz):
        return OWN_CORE.index(Q_PLACE[dz, 0])

    for i, (target, hop) in enumerate(((-3, -1), (3, 1), (4, -2 * zsig))):
        zs1[i] = zp[z_part(target)].astype(BF16)
        send(zs1.at[i], zr1.at[i], z1_ss.at[i], z1_rs.at[i], dev(0, 0, hop, 0))
    for i, target in ((2, -1), (3, 1)):
        zs2[i] = zp[z_part(target)].astype(BF16)
        send(zs2.at[i], zr2.at[i], z2_ss.at[i], z2_rs.at[i], dev(0, 0, target, 0))

    dc_group(2)
    for slot in (11, 12, 10):
        dc_send(slot)
    dc_group(1)
    for slot in (7, 8, 9):
        dc_send(slot)
    dc_group(0)
    for i, (slot, there, even, odd) in enumerate(
        (
            (c_slot(6, 3), c_slot(6, 3), (0, 2), (2, 0)),
            (c_slot(1, 4), c_slot(2, 5), (1, 0), (0, 1)),
            (c_slot(2, 5), c_slot(1, 4), (3, 0), (0, 3)),
        )
    ):
        xs2[i] = dcf[slot].astype(BF16)
        to = dev(even[0] + par * (odd[0] - even[0]), even[1] + par * (odd[1] - even[1]), 0, 0)
        send(xs2.at[i], xr2.at[there - 1], x2_ss.at[i], x2_rs.at[there - 1], to)

    for i in range(3):
        arrived(zr1.at[i], z1_ss.at[i], z1_rs.at[i])
    far = zr1[2].astype(F32)
    down = zp[z_part(-2)] + zr1[0].astype(F32) + jnp.where(zpar == 0, far, 0.0)
    up = zp[z_part(2)] + zr1[1].astype(F32) + jnp.where(zpar == 1, far, 0.0)
    zs2[0] = down.astype(BF16)
    zs2[1] = up.astype(BF16)
    send(zs2.at[0], zr2.at[0], z2_ss.at[0], z2_rs.at[0], dev(0, 0, -2, 0))
    send(zs2.at[1], zr2.at[1], z2_ss.at[1], z2_rs.at[1], dev(0, 0, 2, 0))

    for j, (slot, there, even, odd) in enumerate(
        (
            (c_slot(3, 6), c_slot(3, 6), (2, 0), (0, 2)),
            (c_slot(4, 1), c_slot(5, 2), (0, 1), (1, 0)),
            (c_slot(5, 2), c_slot(4, 1), (0, 3), (3, 0)),
        )
    ):
        total = dcf[slot]
        for d in range(3):
            arrived(xr1.at[3 * j + d], x1_ss.at[3 * j + d], x1_rs.at[3 * j + d])
            total = total + xr1[3 * j + d].astype(F32)
        xs2[3 + j] = total.astype(BF16)
        to = dev(even[0] + par * (odd[0] - even[0]), even[1] + par * (odd[1] - even[1]), 0, 0)
        send(xs2.at[3 + j], xr2.at[there - 1], x2_ss.at[3 + j], x2_rs.at[there - 1], to)

    total = zp[0]
    for i in (2, 3, 0, 1):
        arrived(zr2.at[i], z2_ss.at[i], z2_rs.at[i])
        total = total + zr2[i].astype(F32)
    dq_out[...] = (total * cot[0:1, :]).T
    total = dcf[0]
    for i in range(6):
        arrived(xr2.at[i], x2_ss.at[i], x2_rs.at[i])
        total = total + xr2[i].astype(F32)
    dc_out[...] = total
    for copy in pending:
        copy.wait_send()


def shards(queries, candidates, block_mask, row_class, col_class, cotangent):
    dma = pltpu.SemaphoreType.DMA
    vmem = pltpu.VMEM
    block = (D, ROWS)
    scratch = [
        vmem((NB, NB), jnp.int32),
        vmem((NB, ROWS), jnp.int32),
        vmem((NB, ROWS), jnp.int32),
        vmem((NX, ROWS), F32),
        vmem((SLOTS, 8, ROWS), F32),
        vmem((SLOTS, ROWS, D), BF16),
        vmem((SLOTS, ROWS, D), BF16),
        vmem((D, TILE), BF16),
        vmem((TILE, TILE), BF16),
        vmem((8, TILE), F32),
        vmem((8, TILE), F32),
        vmem((NB, TILE), BF16),
        vmem((TILE, NB), BF16),
        vmem((8,) + block, F32),
        vmem((8,) + block, F32),
        vmem((32, ROWS), F32),
        vmem((32, ROWS), F32),
        vmem((NZ, 32, ROWS), F32),
        vmem((32, ROWS), F32),
        vmem((2, D, TILE), BF16),
        vmem((SLOTS, ROWS, D), F32),
        vmem((2, 4, 2 * D, ROWS), BF16),
        vmem((2, 4, 2 * D, ROWS), BF16),
        vmem((8,) + block, F32),
        vmem((3,) + block, BF16),
        vmem((3,) + block, BF16),
        vmem((4,) + block, BF16),
        vmem((4,) + block, BF16),
        vmem((9, ROWS, D), BF16),
        vmem((9, ROWS, D), BF16),
        vmem((6, ROWS, D), BF16),
        vmem((6, ROWS, D), BF16),
        dma((6,)),
        dma((7,)), dma((7,)), dma((8,)), dma((8,)), dma((7,)), dma((7,)), dma((8,)), dma((8,)),
        dma((16,)), dma((16,)), dma((8,)), dma((8,)), dma((2,)), dma((2,)),
        dma((3,)), dma((3,)), dma((4,)), dma((4,)), dma((9,)), dma((9,)), dma((6,)), dma((6,)),
    ]
    out = vmem((ROWS, D), F32)
    dq, dc = pl.pallas_call(
        kernel,
        out_shape=(out, out),
        in_specs=[pl.BlockSpec(memory_space=pl.ANY)] * 6,
        out_specs=(pl.BlockSpec(memory_space=vmem), pl.BlockSpec(memory_space=vmem)),
        scratch_shapes=scratch,
        compiler_params=pltpu.CompilerParams(
            collective_id=0, has_side_effects=True, vmem_limit_bytes=56 * 2**20
        ),
    )(
        queries,
        candidates,
        block_mask,
        row_class.reshape(NB, ROWS),
        col_class.reshape(NB, ROWS),
        cotangent.reshape(NX, ROWS),
    )
    scale = 1.0 / math.sqrt(D)
    return dq * scale, dc * scale


def solution(mesh):
    in_specs = (P(("row", "col"), None), P(("row", "col"), None), P(), P(), P(), P("row"))
    out_specs = (P(("row", "col"), None), P(("row", "col"), None))
    return jax.shard_map(shards, mesh=mesh, in_specs=in_specs, out_specs=out_specs, check_vma=False)
```

time: 55.2 us -> 49.3 us (0.89)
  Pallas kernels: 52.2 us -> 47.8 us
  local copies, waits for them, and re-layouts: 2.26 us -> 0 us
  other arithmetic: 0 us -> 0.72 us
    pallas_call x1, Pallas kernels: 52.2 us -> 47.8 us  [shards(): pl.pallas_call(kernel, out_shape=(out, out), in_specs=[pl.BlockSpec(memor...]
    unnamed x4 -> x0, local copies, waits for them, and re-layouts: 2.26 us -> none
    mul x0 -> x1, other arithmetic: none -> 0.72 us  [shards(): return (dq * scale, dc * scale)]
where the time goes in v2:
time: 49.3 us; the launch traced here: 49.2 us
  Pallas kernels  47.8 us (97%)
  other arithmetic  0.72 us (1%)
  between operations  0.64 us (1%)
    pallas_call x1, Pallas kernels, shards(): pl.pallas_call(kernel, out_shape=(out, out), in_specs=[pl.BlockSpec(memor...  47.8 us

profile of v2, /device:TPU:1, one launch (start us, length us, event | category | flops | bytes accessed | tf_op | source)
XLA Modules:
  0.0 49.2 jit_solution(7995816153947204990)
XLA Ops:
  0.6 47.8 %shard_map.77 = (f32[128,256]{1,0:T(8,128)S(1)}, f32[128,256]{1,0:T(8,128)S(1)}) custom-call(bf16[128,256]{1,0:T(8,128)(2,1)} %q_own.1, bf16[128,256]{1,0:T(8,128)(2,1)} %c_own.1, s32[256,256]{1,0:T(8,128)} %mask_hbm.1, s32[256,128]{1,0:T(8,128)} %bitcast.3, s32[256,128]{1,0:T(8,128)} %bitcast.4, f32[4,128]{1,0:T(4,128)} %bitcast.5), custom_call_target="tpu_custom_call" | custom-call | tf_op jit(solution)/shard_map/pallas_call | solution.py:493
  48.5 0.7 %broadcast_multiply_fusion = (f32[128,256]{1,0:T(8,128)}, f32[128,256]{1,0:T(8,128)}) fusion(f32[128,256]{1,0:T(8,128)S(1)} %get-tuple-element.5, f32[128,256]{1,0:T(8,128)S(1)} %get-tuple-element.4), kind=kLoop, calls=%fused_computation | loop fusion | flops 65536 | bytes 524288 | tf_op jit(solution)/shard_map/mul | solution.py:511

commit v3 on v2

--- a/solution.py
+++ b/solution.py
@@ -24,7 +24,7 @@
 OFFSETS = [(0, 0), (1, 0), (3, 0), (2, 0), (0, 1), (0, 3), (0, 2)]
 OFFSETS += [(1, 1), (1, 3), (3, 1), (3, 3), (1, 2), (3, 2), (2, 1), (2, 3), (2, 2)]
 PLACE = {o: i for i, o in enumerate(OFFSETS)}
-GROUPS = ((0, 7), (7, 10), (10, 13), (13, 16))
+GROUPS = ((0, 7), (7, 11), (11, 16))
 Q_OFFSETS = [(0, 0), (-2, 0), (2, 0), (-1, 0), (0, 1), (-2, 1), (2, 1), (-1, 1)]
 Q_OFFSETS += [(1, 0), (4, 0), (-3, 0), (3, 0), (1, 1), (4, 1), (-3, 1), (3, 1)]
 Q_PLACE = {o: i for i, o in enumerate(Q_OFFSETS)}
@@ -48,9 +48,9 @@
     q_own, c_own, mask_hbm, rc_hbm, cc_hbm, cot_hbm, dq_out, dc_out,
     mask_ref, rc_ref, cc_ref, cot_ref, aux,
     qg, cg, qt, e, m_ref, l_ref, pt, pc, ot, post, st_own, st_sib, st_all, st_end, aqt,
-    dcf, zs_sib, zr_sib, zp, zs1, zr1, zs2, zr2, xs1, xr1, xs2, xr2,
+    dcf, zs_sib, zr_sib, zp, zs1, zr1, zs2, zr2, xs1, xr1, xs2, xr2, xs3, xr3,
     in_s, q_ss, q_rs, qf_ss, qf_rs, a_ss, a_rs, af_ss, af_rs, c_ss, c_rs, t_ss, t_rs, zb_ss, zb_rs,
-    z1_ss, z1_rs, z2_ss, z2_rs, x1_ss, x1_rs, x2_ss, x2_rs,
+    z1_ss, z1_rs, z2_ss, z2_rs, x1_ss, x1_rs, x2_ss, x2_rs, x3_ss, x3_rs,
 ):
     kk = LOG2E / math.sqrt(D)
     x = lax.axis_index("col")
@@ -232,56 +232,59 @@
         scores = lax.dot_general(c_rows, q_rows, NT, preferred_element_type=F32)
         top = jnp.max(scores, axis=0, keepdims=True)
         grown = jnp.exp2((scores - top) * kk)
-        m_ref[g : g + 1, lanes] = top
+        m_ref[g : g + 1, lanes] = top * kk
         l_ref[g : g + 1, lanes] = jnp.sum(grown, axis=0, keepdims=True)
         e[rows, lanes] = grown.astype(BF16)
+
+    def c_wait(g):
+        for slot in range(*GROUPS[g]):
+            arrived(cg.at[slot], c_ss.at[slot], c_rs.at[slot])
 
     wave(0, 0, 4)
     for i, dz in ((7, 0), (0, -2), (1, 2), (2, -1)):
         slot = Q_PLACE[dz, 1]
         arrived(qg.at[slot], qf_ss.at[i], qf_rs.at[i])
     wave(0, 4, 8)
+    c_wait(1)
+    wave(1, 0, 8)
     for i, dz in ((5, -3), (6, 3), (4, 4)):
         q_arrived(i, dz)
         q_pass(i, dz)
     wave(0, 8, 12)
+    wave(1, 8, 12)
     for i, dz in ((4, 4), (5, -3), (6, 3)):
         a_pass(i, dz)
+    c_wait(2)
+    wave(2, 0, 12)
     for i, dz in ((3, 1), (5, -3), (6, 3), (4, 4)):
         slot = Q_PLACE[dz, 1]
         arrived(qg.at[slot], qf_ss.at[i], qf_rs.at[i])
-    wave(0, 12, 16)
-    for g in (1, 2, 3):
-        for slot in range(*GROUPS[g]):
-            arrived(cg.at[slot], c_ss.at[slot], c_rs.at[slot])
-        wave(g, 0, 16)
-    m_groups = m_ref[0:4, :]
-    m_tile = jnp.max(m_groups, axis=0, keepdims=True)
-    l_tile = jnp.sum(l_ref[0:4, :] * jnp.exp2((m_groups - m_tile) * kk), axis=0, keepdims=True)
+    for g in range(3):
+        wave(g, 12, 16)
+    tops = m_ref[0:3, :]
+    top_tile = jnp.max(tops, axis=0, keepdims=True)
+    mass = jnp.sum(l_ref[0:3, :] * jnp.exp2(tops - top_tile), axis=0, keepdims=True)
+    log_tile = top_tile + jnp.log2(mass)
 
     places = [2 * ((z + dz) % NZ) + (core + dc) % 2 for dz, dc in Q_OFFSETS]
 
-    def slot_rows(ref, start):
-        return as_row([ref[pl.ds(start + place, 1), :] for place in places])
+    def slot_rows(ref):
+        return as_row([ref[pl.ds(place, 1), :] for place in places])
 
     for s, place in enumerate(places):
-        st_own[pl.ds(place, 1), :] = m_tile[:, lanes_of(s)]
-        st_own[pl.ds(SLOTS + place, 1), :] = l_tile[:, lanes_of(s)]
+        st_own[pl.ds(place, 1), :] = log_tile[:, lanes_of(s)]
     send(st_own, st_sib, t_ss.at[0], t_rs.at[0], sibling)
     for s in range(SLOTS):
         qt[:, lanes_of(s)] = qg[s].T
     arrived(st_sib, t_ss.at[0], t_rs.at[0])
-    m_a, m_b = st_own[0:SLOTS, :], st_sib[0:SLOTS, :]
-    m_pair = jnp.maximum(m_a, m_b)
-    l_pair = st_own[SLOTS:32, :] * jnp.exp2((m_a - m_pair) * kk)
-    l_pair = l_pair + st_sib[SLOTS:32, :] * jnp.exp2((m_b - m_pair) * kk)
-    st_all[z, 0:SLOTS, :] = m_pair
-    st_all[z, SLOTS:32, :] = l_pair
+    log_a, log_b = st_own[...], st_sib[...]
+    top = jnp.maximum(log_a, log_b)
+    st_all[z] = top + jnp.log2(jnp.exp2(log_a - top) + jnp.exp2(log_b - top))
     for d in (4, 3, 5, 2, 6, 1, 7):
         send(st_all.at[z], st_all.at[z], t_ss.at[d], t_rs.at[d], dev(0, 0, d, 0))
 
-    m_pair_row = slot_rows(st_all.at[z], 0)
-    shrink = jnp.exp2((m_groups - m_pair_row) * kk)
+    log_pair = slot_rows(st_all.at[z])
+    shrink = jnp.exp2(tops - log_pair)
     own_class = [
         jnp.where((cc[b : b + 1, :] == class_of) & (slot_of == b), 1.0, 0.0).astype(BF16) for b in range(SLOTS)
     ]
@@ -334,18 +337,34 @@
     for d in (1, 7, 2, 6, 3, 5, 4):
         slot = (z - d + NZ) % NZ
         arrived(st_all.at[slot], t_ss.at[d], t_rs.at[d])
-    m_all = st_all[0, 0:SLOTS, :]
+    top = st_all[0]
     for s in range(1, NZ):
-        m_all = jnp.maximum(m_all, st_all[s, 0:SLOTS, :])
-    l_all = jnp.zeros((SLOTS, ROWS), F32)
+        top = jnp.maximum(top, st_all[s])
+    mass = jnp.zeros((SLOTS, ROWS), F32)
     for s in range(NZ):
-        l_all = l_all + st_all[s, SLOTS:32, :] * jnp.exp2((st_all[s, 0:SLOTS, :] - m_all) * kk)
-    st_end[0:SLOTS, :] = m_all
-    st_end[SLOTS:32, :] = 1.0 / l_all
-    top_row, per_mass = slot_rows(st_end, 0), slot_rows(st_end, SLOTS)
-    soft_row = soft_row * per_mass
-    a_groups = soft_row * cot_row * jnp.exp2((m_groups - top_row) * kk)
-    a_pair = soft_row * jnp.exp2((m_pair_row - top_row) * kk)
+        mass = mass + jnp.exp2(st_all[s] - top)
+    st_end[0] = top
+    st_end[1] = 1.0 / mass
+    top_row = slot_rows(st_end.at[0])
+    soft_row = soft_row * slot_rows(st_end.at[1])
+    a_groups = soft_row * cot_row * jnp.exp2(tops - top_row)
+    a_pair = soft_row * jnp.exp2(log_pair - top_row)
+
+    def z_part(dz):
+        return OWN_CORE.index(Q_PLACE[dz, 0])
+
+    def z_sum(i):
+        s = OWN_CORE[i]
+        half, j = i // 4, i % 4
+        soft = ot[i] + zr_sib[half, j, 0:D, :].astype(F32)
+        hits = post[i] + zr_sib[half, j, D : 2 * D, :].astype(F32)
+        return soft * a_pair[:, lanes_of(s)] - hits * per_count[s : s + 1, :]
+
+    for half in range(2):
+        arrived(zr_sib.at[half], zb_ss.at[half], zb_rs.at[half])
+    for i, (target, hop) in enumerate(((4, -2 * zsig), (-3, -1), (3, 1))):
+        zs1[i] = z_sum(z_part(target)).astype(BF16)
+        send(zs1.at[i], zr1.at[i], z1_ss.at[i], z1_rs.at[i], dev(0, 0, hop, 0))
 
     def dc_group(g):
         first, last = GROUPS[g]
@@ -359,7 +378,7 @@
 
     def dc_send(slot):
         a, b = OFFSETS[slot]
-        i = slot - 7
+        i = slot - 11
         odd = (par + a + b) % 2
         xs1[i] = dcf[slot].astype(BF16)
         even_to = hub[a] * 3 + (-b) % NY - 1
@@ -367,35 +386,20 @@
         there = even_to + odd * (odd_to - even_to)
         send(xs1.at[i], xr1.at[there], x1_ss.at[i], x1_rs.at[there], dev(odd * a, (1 - odd) * b, 0, 0))
 
-    dc_group(3)
-    for slot in (15, 13, 14):
+    dc_group(2)
+    for slot in (15, 11, 12, 13, 14):
         dc_send(slot)
-
-    for half in range(2):
-        arrived(zr_sib.at[half], zb_ss.at[half], zb_rs.at[half])
-    for i, s in enumerate(OWN_CORE):
-        lanes = lanes_of(s)
-        half, j = i // 4, i % 4
-        soft = ot[i] + zr_sib[half, j, 0:D, :].astype(F32)
-        hits = post[i] + zr_sib[half, j, D : 2 * D, :].astype(F32)
-        zp[i] = soft * a_pair[:, lanes] - hits * per_count[s : s + 1, :]
-
-    def z_part(dz):
-        return OWN_CORE.index(Q_PLACE[dz, 0])
-
-    for i, (target, hop) in enumerate(((-3, -1), (3, 1), (4, -2 * zsig))):
-        zs1[i] = zp[z_part(target)].astype(BF16)
-        send(zs1.at[i], zr1.at[i], z1_ss.at[i], z1_rs.at[i], dev(0, 0, hop, 0))
     for i, target in ((2, -1), (3, 1)):
-        zs2[i] = zp[z_part(target)].astype(BF16)
+        zs2[i] = z_sum(z_part(target)).astype(BF16)
         send(zs2.at[i], zr2.at[i], z2_ss.at[i], z2_rs.at[i], dev(0, 0, target, 0))
-
-    dc_group(2)
-    for slot in (11, 12, 10):
-        dc_send(slot)
     dc_group(1)
-    for slot in (7, 8, 9):
-        dc_send(slot)
+    for slot in range(7, 11):
+        a, b = OFFSETS[slot]
+        back = PLACE[(-a) % NX, (-b) % NY] - 7
+        xs3[slot - 7] = dcf[slot].astype(BF16)
+        send(xs3.at[slot - 7], xr3.at[back], x3_ss.at[back], x3_rs.at[back], dev(a, b, 0, 0))
+    for target in (0, -2, 2):
+        zp[z_part(target)] = z_sum(z_part(target))
     dc_group(0)
     for i, (slot, there, even, odd) in enumerate(
         (
@@ -410,9 +414,9 @@
 
     for i in range(3):
         arrived(zr1.at[i], z1_ss.at[i], z1_rs.at[i])
-    far = zr1[2].astype(F32)
-    down = zp[z_part(-2)] + zr1[0].astype(F32) + jnp.where(zpar == 0, far, 0.0)
-    up = zp[z_part(2)] + zr1[1].astype(F32) + jnp.where(zpar == 1, far, 0.0)
+    far = zr1[0].astype(F32)
+    down = zp[z_part(-2)] + zr1[1].astype(F32) + jnp.where(zpar == 0, far, 0.0)
+    up = zp[z_part(2)] + zr1[2].astype(F32) + jnp.where(zpar == 1, far, 0.0)
     zs2[0] = down.astype(BF16)
     zs2[1] = up.astype(BF16)
     send(zs2.at[0], zr2.at[0], z2_ss.at[0], z2_rs.at[0], dev(0, 0, -2, 0))
@@ -426,8 +430,8 @@
         )
     ):
         total = dcf[slot]
-        for d in range(3):
-            arrived(xr1.at[3 * j + d], x1_ss.at[3 * j + d], x1_rs.at[3 * j + d])
+        for d in range(3) if j == 0 else (1,):
+            arrived(xr1.at[3 * j + d], x1_ss.at[0], x1_rs.at[3 * j + d])
             total = total + xr1[3 * j + d].astype(F32)
         xs2[3 + j] = total.astype(BF16)
         to = dev(even[0] + par * (odd[0] - even[0]), even[1] + par * (odd[1] - even[1]), 0, 0)
@@ -442,6 +446,9 @@
     for i in range(6):
         arrived(xr2.at[i], x2_ss.at[i], x2_rs.at[i])
         total = total + xr2[i].astype(F32)
+    for i in range(4):
+        arrived(xr3.at[i], x3_ss.at[i], x3_rs.at[i])
+        total = total + xr3[i].astype(F32)
     dc_out[...] = total
     for copy in pending:
         copy.wait_send()
@@ -467,10 +474,10 @@
         vmem((TILE, NB), BF16),
         vmem((8,) + block, F32),
         vmem((8,) + block, F32),
-        vmem((32, ROWS), F32),
-        vmem((32, ROWS), F32),
-        vmem((NZ, 32, ROWS), F32),
-        vmem((32, ROWS), F32),
+        vmem((SLOTS, ROWS), F32),
+        vmem((SLOTS, ROWS), F32),
+        vmem((NZ, SLOTS, ROWS), F32),
+        vmem((2, SLOTS, ROWS), F32),
         vmem((2, D, TILE), BF16),
         vmem((SLOTS, ROWS, D), F32),
         vmem((2, 4, 2 * D, ROWS), BF16),
@@ -480,14 +487,16 @@
         vmem((3,) + block, BF16),
         vmem((4,) + block, BF16),
         vmem((4,) + block, BF16),
-        vmem((9, ROWS, D), BF16),
+        vmem((5, ROWS, D), BF16),
         vmem((9, ROWS, D), BF16),
         vmem((6, ROWS, D), BF16),
         vmem((6, ROWS, D), BF16),
+        vmem((4, ROWS, D), BF16),
+        vmem((4, ROWS, D), BF16),
         dma((6,)),
         dma((7,)), dma((7,)), dma((8,)), dma((8,)), dma((7,)), dma((7,)), dma((8,)), dma((8,)),
         dma((16,)), dma((16,)), dma((8,)), dma((8,)), dma((2,)), dma((2,)),
-        dma((3,)), dma((3,)), dma((4,)), dma((4,)), dma((9,)), dma((9,)), dma((6,)), dma((6,)),
+        dma((3,)), dma((3,)), dma((4,)), dma((4,)), dma((5,)), dma((9,)), dma((6,)), dma((6,)), dma((4,)), dma((4,)),
     ]
     out = vmem((ROWS, D), F32)
     dq, dc = pl.pallas_call(

time: 49.3 us -> 47 us (0.953)
  Pallas kernels: 47.8 us -> 45.3 us
    pallas_call x1, Pallas kernels: 47.8 us -> 45.3 us  [shards(): pl.pallas_call(kernel, out_shape=(out, out), in_specs=[pl.BlockSpec(memor...]
where the time goes in v3:
time: 47 us; the launch traced here: 46.6 us
  Pallas kernels  45.3 us (96%)
  other arithmetic  0.72 us (2%)
  between operations  0.64 us (1%)
    pallas_call x1, Pallas kernels, shards(): pl.pallas_call(kernel, out_shape=(out, out), in_specs=[pl.BlockSpec(memor...  45.3 us

profile of v3, /device:TPU:1, one launch (start us, length us, event | category | flops | bytes accessed | tf_op | source)
XLA Modules:
  0.0 46.6 jit_solution(2103652860945076976)
XLA Ops:
  0.6 45.3 %shard_map.77 = (f32[128,256]{1,0:T(8,128)S(1)}, f32[128,256]{1,0:T(8,128)S(1)}) custom-call(bf16[128,256]{1,0:T(8,128)(2,1)} %q_own.1, bf16[128,256]{1,0:T(8,128)(2,1)} %c_own.1, s32[256,256]{1,0:T(8,128)} %mask_hbm.1, s32[256,128]{1,0:T(8,128)} %bitcast.3, s32[256,128]{1,0:T(8,128)} %bitcast.4, f32[4,128]{1,0:T(4,128)} %bitcast.5), custom_call_target="tpu_custom_call" | custom-call | tf_op jit(solution)/shard_map/pallas_call | solution.py:502
  45.9 0.7 %broadcast_multiply_fusion = (f32[128,256]{1,0:T(8,128)}, f32[128,256]{1,0:T(8,128)}) fusion(f32[128,256]{1,0:T(8,128)S(1)} %get-tuple-element.5, f32[128,256]{1,0:T(8,128)S(1)} %get-tuple-element.4), kind=kLoop, calls=%fused_computation | loop fusion | flops 65536 | bytes 524288 | tf_op jit(solution)/shard_map/mul | solution.py:520

commit v4 on v3

--- a/solution.py
+++ b/solution.py
@@ -48,9 +48,9 @@
     q_own, c_own, mask_hbm, rc_hbm, cc_hbm, cot_hbm, dq_out, dc_out,
     mask_ref, rc_ref, cc_ref, cot_ref, aux,
     qg, cg, qt, e, m_ref, l_ref, pt, pc, ot, post, st_own, st_sib, st_all, st_end, aqt,
-    dcf, zs_sib, zr_sib, zp, zs1, zr1, zs2, zr2, xs1, xr1, xs2, xr2, xs3, xr3,
+    dcf, zs_sib, zr_sib, zp, zs1, zr1, zs2, zr2, xs1, xr1, xs2, xr2,
     in_s, q_ss, q_rs, qf_ss, qf_rs, a_ss, a_rs, af_ss, af_rs, c_ss, c_rs, t_ss, t_rs, zb_ss, zb_rs,
-    z1_ss, z1_rs, z2_ss, z2_rs, x1_ss, x1_rs, x2_ss, x2_rs, x3_ss, x3_rs,
+    z1_ss, z1_rs, z2_ss, z2_rs, x1_ss, x1_rs, x2_ss, x2_rs,
 ):
     kk = LOG2E / math.sqrt(D)
     x = lax.axis_index("col")
@@ -374,44 +374,39 @@
         part = part + jnp.dot(pc[rows, :], sums_q, preferred_element_type=F32)
         dcf[first:last] = part.reshape(last - first, ROWS, D)
 
-    hub = {2: 0, 1: 1, 3: 2}
-
-    def dc_send(slot):
-        a, b = OFFSETS[slot]
-        i = slot - 11
-        odd = (par + a + b) % 2
+    def dc_send(slot, dx, dy):
+        i = slot - 7
         xs1[i] = dcf[slot].astype(BF16)
-        even_to = hub[a] * 3 + (-b) % NY - 1
-        odd_to = hub[b] * 3 + (-a) % NX - 1
-        there = even_to + odd * (odd_to - even_to)
-        send(xs1.at[i], xr1.at[there], x1_ss.at[i], x1_rs.at[there], dev(odd * a, (1 - odd) * b, 0, 0))
+        send(xs1.at[i], xr1.at[i], x1_ss.at[i], x1_rs.at[i], dev(dx, dy, 0, 0))
+
+    def dc_hub(o, *others):
+        total = dcf[PLACE[o]]
+        for other in others:
+            total = total + xr1[PLACE[other] - 7].astype(F32)
+        if o in ((2, 0), (0, 2)):
+            total = total + jnp.where(par == o[0] // 2, xr1[PLACE[2, 2] - 7].astype(F32), 0.0)
+        i = PLACE[o] - 1
+        xs2[i] = total.astype(BF16)
+        send(xs2.at[i], xr2.at[i], x2_ss.at[i], x2_rs.at[i], dev(o[0], o[1], 0, 0))
+
+    def dc_wait(*slots):
+        for o in slots:
+            i = PLACE[o] - 7
+            arrived(xr1.at[i], x1_ss.at[i], x1_rs.at[i])
 
     dc_group(2)
-    for slot in (15, 11, 12, 13, 14):
-        dc_send(slot)
+    dc_send(PLACE[2, 2], 2 - 2 * par, 2 * par)
+    for o, hop in (((1, 2), (1, 0)), ((2, 1), (0, 1)), ((3, 2), (3, 0)), ((2, 3), (0, 3))):
+        dc_send(PLACE[o], *hop)
     for i, target in ((2, -1), (3, 1)):
         zs2[i] = z_sum(z_part(target)).astype(BF16)
         send(zs2.at[i], zr2.at[i], z2_ss.at[i], z2_rs.at[i], dev(0, 0, target, 0))
     dc_group(1)
-    for slot in range(7, 11):
-        a, b = OFFSETS[slot]
-        back = PLACE[(-a) % NX, (-b) % NY] - 7
-        xs3[slot - 7] = dcf[slot].astype(BF16)
-        send(xs3.at[slot - 7], xr3.at[back], x3_ss.at[back], x3_rs.at[back], dev(a, b, 0, 0))
+    for o, hop in (((1, 1), (1, 0)), ((3, 1), (0, 1)), ((3, 3), (3, 0)), ((1, 3), (0, 3))):
+        dc_send(PLACE[o], *hop)
     for target in (0, -2, 2):
         zp[z_part(target)] = z_sum(z_part(target))
     dc_group(0)
-    for i, (slot, there, even, odd) in enumerate(
-        (
-            (c_slot(6, 3), c_slot(6, 3), (0, 2), (2, 0)),
-            (c_slot(1, 4), c_slot(2, 5), (1, 0), (0, 1)),
-            (c_slot(2, 5), c_slot(1, 4), (3, 0), (0, 3)),
-        )
-    ):
-        xs2[i] = dcf[slot].astype(BF16)
-        to = dev(even[0] + par * (odd[0] - even[0]), even[1] + par * (odd[1] - even[1]), 0, 0)
-        send(xs2.at[i], xr2.at[there - 1], x2_ss.at[i], x2_rs.at[there - 1], to)
-
     for i in range(3):
         arrived(zr1.at[i], z1_ss.at[i], z1_rs.at[i])
     far = zr1[0].astype(F32)
@@ -422,20 +417,13 @@
     send(zs2.at[0], zr2.at[0], z2_ss.at[0], z2_rs.at[0], dev(0, 0, -2, 0))
     send(zs2.at[1], zr2.at[1], z2_ss.at[1], z2_rs.at[1], dev(0, 0, 2, 0))
 
-    for j, (slot, there, even, odd) in enumerate(
-        (
-            (c_slot(3, 6), c_slot(3, 6), (2, 0), (0, 2)),
-            (c_slot(4, 1), c_slot(5, 2), (0, 1), (1, 0)),
-            (c_slot(5, 2), c_slot(4, 1), (0, 3), (3, 0)),
-        )
-    ):
-        total = dcf[slot]
-        for d in range(3) if j == 0 else (1,):
-            arrived(xr1.at[3 * j + d], x1_ss.at[0], x1_rs.at[3 * j + d])
-            total = total + xr1[3 * j + d].astype(F32)
-        xs2[3 + j] = total.astype(BF16)
-        to = dev(even[0] + par * (odd[0] - even[0]), even[1] + par * (odd[1] - even[1]), 0, 0)
-        send(xs2.at[3 + j], xr2.at[there - 1], x2_ss.at[3 + j], x2_rs.at[there - 1], to)
+    dc_wait((2, 2), (2, 1), (2, 3))
+    dc_hub((2, 0), (2, 1), (2, 3))
+    dc_wait((1, 2), (3, 2))
+    dc_hub((0, 2), (1, 2), (3, 2))
+    for o, other in (((0, 1), (1, 1)), ((1, 0), (1, 3)), ((0, 3), (3, 3)), ((3, 0), (3, 1))):
+        dc_wait(other)
+        dc_hub(o, other)
 
     total = zp[0]
     for i in (2, 3, 0, 1):
@@ -446,9 +434,6 @@
     for i in range(6):
         arrived(xr2.at[i], x2_ss.at[i], x2_rs.at[i])
         total = total + xr2[i].astype(F32)
-    for i in range(4):
-        arrived(xr3.at[i], x3_ss.at[i], x3_rs.at[i])
-        total = total + xr3[i].astype(F32)
     dc_out[...] = total
     for copy in pending:
         copy.wait_send()
@@ -487,16 +472,14 @@
         vmem((3,) + block, BF16),
         vmem((4,) + block, BF16),
         vmem((4,) + block, BF16),
-        vmem((5, ROWS, D), BF16),
+        vmem((9, ROWS, D), BF16),
         vmem((9, ROWS, D), BF16),
         vmem((6, ROWS, D), BF16),
         vmem((6, ROWS, D), BF16),
-        vmem((4, ROWS, D), BF16),
-        vmem((4, ROWS, D), BF16),
         dma((6,)),
         dma((7,)), dma((7,)), dma((8,)), dma((8,)), dma((7,)), dma((7,)), dma((8,)), dma((8,)),
         dma((16,)), dma((16,)), dma((8,)), dma((8,)), dma((2,)), dma((2,)),
-        dma((3,)), dma((3,)), dma((4,)), dma((4,)), dma((5,)), dma((9,)), dma((6,)), dma((6,)), dma((4,)), dma((4,)),
+        dma((3,)), dma((3,)), dma((4,)), dma((4,)), dma((9,)), dma((9,)), dma((6,)), dma((6,)),
     ]
     out = vmem((ROWS, D), F32)
     dq, dc = pl.pallas_call(

time: 47 us -> 45.7 us (0.972)
  Pallas kernels: 45.3 us -> 44.2 us
    pallas_call x1, Pallas kernels: 45.3 us -> 44.2 us  [shards(): pl.pallas_call(kernel, out_shape=(out, out), in_specs=[pl.BlockSpec(memor...]
where the time goes in v4:
time: 45.7 us; the launch traced here: 45.6 us
  Pallas kernels  44.2 us (97%)
  other arithmetic  0.72 us (2%)
  between operations  0.64 us (1%)
    pallas_call x1, Pallas kernels, shards(): pl.pallas_call(kernel, out_shape=(out, out), in_specs=[pl.BlockSpec(memor...  44.2 us

profile of v4, /device:TPU:1, one launch (start us, length us, event | category | flops | bytes accessed | tf_op | source)
XLA Modules:
  0.0 45.6 jit_solution(13991389683731475487)
XLA Ops:
  0.6 44.2 %shard_map.77 = (f32[128,256]{1,0:T(8,128)S(1)}, f32[128,256]{1,0:T(8,128)S(1)}) custom-call(bf16[128,256]{1,0:T(8,128)(2,1)} %q_own.1, bf16[128,256]{1,0:T(8,128)(2,1)} %c_own.1, s32[256,256]{1,0:T(8,128)} %mask_hbm.1, s32[256,128]{1,0:T(8,128)} %bitcast.3, s32[256,128]{1,0:T(8,128)} %bitcast.4, f32[4,128]{1,0:T(4,128)} %bitcast.5), custom_call_target="tpu_custom_call" | custom-call | tf_op jit(solution)/shard_map/pallas_call | solution.py:485
  44.9 0.7 %broadcast_multiply_fusion = (f32[128,256]{1,0:T(8,128)}, f32[128,256]{1,0:T(8,128)}) fusion(f32[128,256]{1,0:T(8,128)S(1)} %get-tuple-element.5, f32[128,256]{1,0:T(8,128)S(1)} %get-tuple-element.4), kind=kLoop, calls=%fused_computation | loop fusion | flops 65536 | bytes 524288 | tf_op jit(solution)/shard_map/mul | solution.py:503

commit v5 on v4

--- a/solution.py
+++ b/solution.py
@@ -11,6 +11,7 @@
 F32 = jnp.float32
 BF16 = jnp.bfloat16
 ROWS = 128
+SENT = ROWS + 16
 D = 256
 NX, NY, NZ = 4, 4, 8
 TILE = 2048
@@ -46,10 +47,10 @@
 
 def kernel(
     q_own, c_own, mask_hbm, rc_hbm, cc_hbm, cot_hbm, dq_out, dc_out,
-    mask_ref, rc_ref, cc_ref, cot_ref, aux,
+    mask_ref, rc_ref, cc_ref, cot_ref,
     qg, cg, qt, e, m_ref, l_ref, pt, pc, ot, post, st_own, st_sib, st_all, st_end, aqt,
     dcf, zs_sib, zr_sib, zp, zs1, zr1, zs2, zr2, xs1, xr1, xs2, xr2,
-    in_s, q_ss, q_rs, qf_ss, qf_rs, a_ss, a_rs, af_ss, af_rs, c_ss, c_rs, t_ss, t_rs, zb_ss, zb_rs,
+    in_s, q_ss, q_rs, qf_ss, qf_rs, c_ss, c_rs, t_ss, t_rs, zb_ss, zb_rs,
     z1_ss, z1_rs, z2_ss, z2_rs, x1_ss, x1_rs, x2_ss, x2_rs,
 ):
     kk = LOG2E / math.sqrt(D)
@@ -92,28 +93,43 @@
         pltpu.make_async_copy(src, dst, in_s.at[i])
         for i, (src, dst) in enumerate(
             (
-                (cot_hbm, cot_ref), (mask_hbm, mask_ref), (rc_hbm, rc_ref), (cc_hbm, cc_ref),
-                (q_own, qg.at[0]), (c_own, cg.at[0]),
+                (q_own, qg.at[0, pl.ds(0, ROWS)]), (cot_hbm, cot_ref), (c_own, cg.at[0]),
+                (mask_hbm, mask_ref), (rc_hbm, rc_ref), (cc_hbm, cc_ref),
             )
         )
     ]
     for load in loads:
         load.start()
+    for load in loads[:3]:
+        load.wait()
+    own_cot = cot_ref[pl.ds(x, 1), :]
+    high = own_cot.astype(BF16).astype(F32)
+    middle = (own_cot - high).astype(BF16).astype(F32)
+    low = own_cot - high - middle
+    part_row = lax.broadcasted_iota(jnp.int32, (16, D), 0)
+    parts = jnp.where(part_row == 0, jnp.concatenate([high, middle], axis=1), 0.0)
+    parts = jnp.where(part_row == 1, jnp.concatenate([low, low], axis=1), parts)
+    qg[0, ROWS:SENT, :] = parts.astype(BF16)
     pl.semaphore_wait(barrier, len(peers))
 
     z_hops = (2, -2, 1, -1)
-    for i, hop in enumerate(z_hops):
-        send(q_own, qg.at[Q_PLACE[-hop, 0]], q_ss.at[i], q_rs.at[i], dev(0, 0, hop, 0))
-    for o in OFFSETS[1:7]:
+
+    def q_first(i):
+        hop = z_hops[i]
+        send(qg.at[0], qg.at[Q_PLACE[-hop, 0]], q_ss.at[i], q_rs.at[i], dev(0, 0, hop, 0))
+
+    def c_first(o):
         back = PLACE[(-o[0]) % NX, (-o[1]) % NY]
-        send(c_own, cg.at[back], c_ss.at[back], c_rs.at[back], dev(o[0], o[1], 0, 0))
-    send(q_own, qg.at[Q_PLACE[0, 1]], qf_ss.at[7], qf_rs.at[7], sibling)
-    for load in loads:
+        send(cg.at[0], cg.at[back], c_ss.at[back], c_rs.at[back], dev(o[0], o[1], 0, 0))
+
+    q_first(0)
+    q_first(1)
+    for o in ((2, 0), (0, 2), (1, 0), (0, 1), (3, 0), (0, 3)):
+        c_first(o)
+    q_first(2)
+    q_first(3)
+    for load in loads[3:]:
         load.wait()
-    aux[0] = jnp.broadcast_to(cot_ref[pl.ds(x, 1), :], (8, ROWS))
-    for i, hop in enumerate(z_hops):
-        send(aux.at[0], aux.at[Q_PLACE[-hop, 0]], a_ss.at[i], a_rs.at[i], dev(0, 0, hop, 0))
-    send(aux.at[0], aux.at[Q_PLACE[0, 1]], af_ss.at[7], af_rs.at[7], sibling)
 
     lane256 = lax.broadcasted_iota(jnp.int32, (SLOTS, NB), 1)
     slot256 = lax.broadcasted_iota(jnp.int32, (SLOTS, NB), 0)
@@ -162,73 +178,55 @@
         pc[lanes_of(s), 0:ROWS] = picked
         pc[lanes_of(s), ROWS:NB] = picked
 
-    def c_slot(even, odd):
-        return even + par * (odd - even)
-
-    turn = [
-        (c_slot(4, 1), 1 - par, par, [((d, 0), (0, d)) for d in (1, 3, 2)], ((0, 1), (1, 0))),
-        (c_slot(5, 2), 1 - par, par, [((d, 0), (0, d)) for d in (1, 3, 2)], ((0, 3), (3, 0))),
-        (c_slot(3, 6), par, 1 - par, [((0, d), (d, 0)) for d in (1, 3, 2)], ((2, 0), (0, 2))),
-    ]
-    forwards = [0]
-
-    def c_forward(slot, fx, fy, hops, origin):
-        arrived(cg.at[slot], c_ss.at[slot], c_rs.at[slot])
-        for even, odd in hops:
-            d = max(even)
-            there = [
-                PLACE[((o[0] - h[0]) % NX, (o[1] - h[1]) % NY)] for o, h in zip(origin, (even, odd))
-            ]
-            there = c_slot(*there)
-            i = 7 + forwards[0]
-            send(cg.at[slot], cg.at[there], c_ss.at[i], c_rs.at[there], dev(fx * d, fy * d, 0, 0))
-            forwards[0] += 1
+    def c_here(*offsets):
+        for o in offsets:
+            arrived(cg.at[PLACE[o]], c_ss.at[PLACE[o]], c_rs.at[PLACE[o]])
+
+    def c_forward(o, dx, dy):
+        there = PLACE[(o[0] - dx) % NX, (o[1] - dy) % NY]
+        send(cg.at[PLACE[o]], cg.at[there], c_ss.at[there], c_rs.at[there], dev(dx, dy, 0, 0))
 
     def q_arrived(i, dz):
         slot = Q_PLACE[dz, 0]
         arrived(qg.at[slot], q_ss.at[i], q_rs.at[i])
 
-    def q_pass(i, dz):
-        here, there = Q_PLACE[dz, 0], Q_PLACE[dz, 1]
-        send(qg.at[here], qg.at[there], qf_ss.at[i], qf_rs.at[i], sibling)
-
-    def a_pass(i, dz):
-        here, there = Q_PLACE[dz, 0], Q_PLACE[dz, 1]
-        arrived(aux.at[here], a_ss.at[i], a_rs.at[i])
-        send(aux.at[here], aux.at[there], af_ss.at[i], af_rs.at[i], sibling)
-
-    def onward(ref, ss, rs):
-        far = Q_PLACE[-2, 0] + zpar * (Q_PLACE[2, 0] - Q_PLACE[-2, 0])
-        send(ref.at[far], ref.at[Q_PLACE[4, 0]], ss.at[4], rs.at[4], dev(0, 0, 2 * zsig, 0))
-        send(ref.at[Q_PLACE[-2, 0]], ref.at[Q_PLACE[-3, 0]], ss.at[5], rs.at[5], dev(0, 0, 1, 0))
-        send(ref.at[Q_PLACE[2, 0]], ref.at[Q_PLACE[3, 0]], ss.at[6], rs.at[6], dev(0, 0, -1, 0))
-
-    c_forward(*turn[0])
-    c_forward(*turn[1])
+    def q_pass(i):
+        here, there = qg.at[pl.ds(8 * i, 4)], qg.at[pl.ds(8 * i + 4, 4)]
+        send(here, there, qf_ss.at[i], qf_rs.at[i], sibling)
+
+    def q_passed(i):
+        arrived(qg.at[pl.ds(8 * i + 4, 4)], qf_ss.at[i], qf_rs.at[i])
+
+    q_far = Q_PLACE[-2, 0] + zpar * (Q_PLACE[2, 0] - Q_PLACE[-2, 0])
+    onward = (
+        (4, q_far, Q_PLACE[4, 0], 2 * zsig),
+        (5, Q_PLACE[-2, 0], Q_PLACE[-3, 0], 1),
+        (6, Q_PLACE[2, 0], Q_PLACE[3, 0], -1),
+    )
+
+    c_here((2, 0), (0, 2))
+    for hop in (1, 3):
+        c_forward((2, 0), 0, hop)
+        c_forward((0, 2), hop, 0)
     q_arrived(0, -2)
     q_arrived(1, 2)
-    onward(qg, q_ss, q_rs)
-    c_forward(*turn[2])
-    q_pass(0, -2)
-    q_pass(1, 2)
+    for i, here, there, dz in onward:
+        send(qg.at[here], qg.at[there], q_ss.at[i], q_rs.at[i], dev(0, 0, dz, 0))
+    far = PLACE[2, 0] + par * (PLACE[0, 2] - PLACE[2, 0])
+    there = PLACE[2, 2]
+    send(cg.at[far], cg.at[there], c_ss.at[there], c_rs.at[there], dev(2 * par, 2 - 2 * par, 0, 0))
+    for o, dx, dy in (((0, 1), 3, 0), ((0, 3), 1, 0), ((1, 0), 0, 1), ((3, 0), 0, 3)):
+        c_here(o)
+        c_forward(o, dx, dy)
     q_arrived(2, -1)
-    q_pass(2, -1)
-    q_arrived(3, 1)
-    q_pass(3, 1)
-    a_pass(0, -2)
-    a_pass(1, 2)
-    a_pass(2, -1)
-    a_pass(3, 1)
-    onward(aux, a_ss, a_rs)
-    for slot in (c_slot(1, 4), c_slot(2, 5), c_slot(6, 3)):
-        arrived(cg.at[slot], c_ss.at[slot], c_rs.at[slot])
+    q_pass(0)
 
     def wave(g, q_first, q_last):
         first, last = GROUPS[g]
         rows = slice(first * ROWS, last * ROWS)
         lanes = slice(q_first * ROWS, q_last * ROWS)
         c_rows = cg[first:last].reshape((last - first) * ROWS, D)
-        q_rows = qg[q_first:q_last].reshape((q_last - q_first) * ROWS, D)
+        q_rows = qg[q_first:q_last, 0:ROWS, :].reshape((q_last - q_first) * ROWS, D)
         scores = lax.dot_general(c_rows, q_rows, NT, preferred_element_type=F32)
         top = jnp.max(scores, axis=0, keepdims=True)
         grown = jnp.exp2((scores - top) * kk)
@@ -241,24 +239,18 @@
             arrived(cg.at[slot], c_ss.at[slot], c_rs.at[slot])
 
     wave(0, 0, 4)
-    for i, dz in ((7, 0), (0, -2), (1, 2), (2, -1)):
-        slot = Q_PLACE[dz, 1]
-        arrived(qg.at[slot], qf_ss.at[i], qf_rs.at[i])
+    q_passed(0)
     wave(0, 4, 8)
     c_wait(1)
     wave(1, 0, 8)
-    for i, dz in ((5, -3), (6, 3), (4, 4)):
+    for i, dz in ((3, 1), (5, -3), (6, 3), (4, 4)):
         q_arrived(i, dz)
-        q_pass(i, dz)
+    q_pass(1)
     wave(0, 8, 12)
     wave(1, 8, 12)
-    for i, dz in ((4, 4), (5, -3), (6, 3)):
-        a_pass(i, dz)
     c_wait(2)
     wave(2, 0, 12)
-    for i, dz in ((3, 1), (5, -3), (6, 3), (4, 4)):
-        slot = Q_PLACE[dz, 1]
-        arrived(qg.at[slot], qf_ss.at[i], qf_rs.at[i])
+    q_passed(1)
     for g in range(3):
         wave(g, 12, 16)
     tops = m_ref[0:3, :]
@@ -275,7 +267,7 @@
         st_own[pl.ds(place, 1), :] = log_tile[:, lanes_of(s)]
     send(st_own, st_sib, t_ss.at[0], t_rs.at[0], sibling)
     for s in range(SLOTS):
-        qt[:, lanes_of(s)] = qg[s].T
+        qt[:, lanes_of(s)] = qg[s, 0:ROWS, :].T
     arrived(st_sib, t_ss.at[0], t_rs.at[0])
     log_a, log_b = st_own[...], st_sib[...]
     top = jnp.maximum(log_a, log_b)
@@ -318,17 +310,18 @@
             ot[4 * half + s] = total[:, lanes_of(s)]
             post[4 * half + s] = hits[:, lanes_of(s)]
 
-    for i, dz in ((7, 0), (0, -2), (1, 2), (2, -1), (3, 1), (4, 4), (5, -3), (6, 3)):
-        slot = Q_PLACE[dz, 1]
-        arrived(aux.at[slot], af_ss.at[i], af_rs.at[i])
-    cot = jnp.concatenate([aux[s, 0:1, :] for s in range(SLOTS)], axis=0)
+    cot = []
+    for s in range(SLOTS):
+        parts = qg[s, ROWS:SENT, :].astype(F32)
+        cot.append(parts[0:1, 0:ROWS] + parts[0:1, ROWS:D] + parts[1:2, 0:ROWS])
+    cot = jnp.concatenate(cot, axis=0)
     coef_pos = cot * per_count
     weights = [
         jnp.where((rc[s : s + 1, :] == class_of) & (slot_of == s), -coef_pos[s : s + 1, :], 0.0)
         for s in range(SLOTS)
     ]
     weights = jnp.concatenate(split2(jnp.concatenate(weights, axis=1)), axis=0)
-    sums_q = jnp.dot(weights, qg[...].reshape(TILE, D), preferred_element_type=F32)
+    sums_q = jnp.dot(weights, qg[:, 0:ROWS, :].reshape(TILE, D), preferred_element_type=F32)
     sums_q = sums_q[0:ROWS, :] + sums_q[ROWS:NB, :]
     sums_q = jnp.concatenate(split2(sums_q), axis=0)
     soft_row = as_row([(count * per_count)[s : s + 1, :] for s in range(SLOTS)])
@@ -362,9 +355,6 @@
 
     for half in range(2):
         arrived(zr_sib.at[half], zb_ss.at[half], zb_rs.at[half])
-    for i, (target, hop) in enumerate(((4, -2 * zsig), (-3, -1), (3, 1))):
-        zs1[i] = z_sum(z_part(target)).astype(BF16)
-        send(zs1.at[i], zr1.at[i], z1_ss.at[i], z1_rs.at[i], dev(0, 0, hop, 0))
 
     def dc_group(g):
         first, last = GROUPS[g]
@@ -394,6 +384,9 @@
             i = PLACE[o] - 7
             arrived(xr1.at[i], x1_ss.at[i], x1_rs.at[i])
 
+    for i, (target, hop) in enumerate(((4, -2 * zsig), (-3, -1), (3, 1))):
+        zs1[i] = z_sum(z_part(target)).astype(BF16)
+        send(zs1.at[i], zr1.at[i], z1_ss.at[i], z1_rs.at[i], dev(0, 0, hop, 0))
     dc_group(2)
     dc_send(PLACE[2, 2], 2 - 2 * par, 2 * par)
     for o, hop in (((1, 2), (1, 0)), ((2, 1), (0, 1)), ((3, 2), (3, 0)), ((2, 3), (0, 3))):
@@ -448,8 +441,7 @@
         vmem((NB, ROWS), jnp.int32),
         vmem((NB, ROWS), jnp.int32),
         vmem((NX, ROWS), F32),
-        vmem((SLOTS, 8, ROWS), F32),
-        vmem((SLOTS, ROWS, D), BF16),
+        vmem((SLOTS, SENT, D), BF16),
         vmem((SLOTS, ROWS, D), BF16),
         vmem((D, TILE), BF16),
         vmem((TILE, TILE), BF16),
@@ -477,7 +469,7 @@
         vmem((6, ROWS, D), BF16),
         vmem((6, ROWS, D), BF16),
         dma((6,)),
-        dma((7,)), dma((7,)), dma((8,)), dma((8,)), dma((7,)), dma((7,)), dma((8,)), dma((8,)),
+        dma((7,)), dma((7,)), dma((2,)), dma((2,)),
         dma((16,)), dma((16,)), dma((8,)), dma((8,)), dma((2,)), dma((2,)),
         dma((3,)), dma((3,)), dma((4,)), dma((4,)), dma((9,)), dma((9,)), dma((6,)), dma((6,)),
     ]

time: 45.7 us -> 44.2 us (0.967)
  Pallas kernels: 44.2 us -> 42.8 us
    pallas_call x1, Pallas kernels: 44.2 us -> 42.8 us  [shards(): pl.pallas_call(kernel, out_shape=(out, out), in_specs=[pl.BlockSpec(memor...]
where the time goes in v5:
time: 44.2 us; the launch traced here: 44.1 us
  Pallas kernels  42.8 us (97%)
  other arithmetic  0.72 us (2%)
  between operations  0.64 us (1%)
    pallas_call x1, Pallas kernels, shards(): pl.pallas_call(kernel, out_shape=(out, out), in_specs=[pl.BlockSpec(memor...  42.8 us

profile of v5, /device:TPU:1, one launch (start us, length us, event | category | flops | bytes accessed | tf_op | source)
XLA Modules:
  0.0 44.1 jit_solution(1271856500258595066)
XLA Ops:
  0.6 42.8 %shard_map.77 = (f32[128,256]{1,0:T(8,128)S(1)}, f32[128,256]{1,0:T(8,128)S(1)}) custom-call(bf16[128,256]{1,0:T(8,128)(2,1)} %q_own.1, bf16[128,256]{1,0:T(8,128)(2,1)} %c_own.1, s32[256,256]{1,0:T(8,128)} %mask_hbm.1, s32[256,128]{1,0:T(8,128)} %bitcast.3, s32[256,128]{1,0:T(8,128)} %bitcast.4, f32[4,128]{1,0:T(4,128)} %bitcast.5), custom_call_target="tpu_custom_call" | custom-call | tf_op jit(solution)/shard_map/pallas_call | solution.py:477
  43.4 0.7 %broadcast_multiply_fusion = (f32[128,256]{1,0:T(8,128)}, f32[128,256]{1,0:T(8,128)}) fusion(f32[128,256]{1,0:T(8,128)S(1)} %get-tuple-element.5, f32[128,256]{1,0:T(8,128)S(1)} %get-tuple-element.4), kind=kLoop, calls=%fused_computation | loop fusion | flops 65536 | bytes 524288 | tf_op jit(solution)/shard_map/mul | solution.py:495

commit v6 on v5

--- a/solution.py
+++ b/solution.py
@@ -122,12 +122,10 @@
         back = PLACE[(-o[0]) % NX, (-o[1]) % NY]
         send(cg.at[0], cg.at[back], c_ss.at[back], c_rs.at[back], dev(o[0], o[1], 0, 0))
 
-    q_first(0)
-    q_first(1)
+    for i in range(4):
+        q_first(i)
     for o in ((2, 0), (0, 2), (1, 0), (0, 1), (3, 0), (0, 3)):
         c_first(o)
-    q_first(2)
-    q_first(3)
     for load in loads[3:]:
         load.wait()
 
@@ -246,10 +244,10 @@
     for i, dz in ((3, 1), (5, -3), (6, 3), (4, 4)):
         q_arrived(i, dz)
     q_pass(1)
-    wave(0, 8, 12)
-    wave(1, 8, 12)
     c_wait(2)
-    wave(2, 0, 12)
+    wave(2, 0, 8)
+    for g in range(3):
+        wave(g, 8, 12)
     q_passed(1)
     for g in range(3):
         wave(g, 12, 16)

time: 44.2 us -> 43.9 us (level)
  no operation moved by 1% of the time
where the time goes in v6:
time: 43.9 us; the launch traced here: 43.8 us
  Pallas kernels  42.5 us (97%)
  other arithmetic  0.72 us (2%)
  between operations  0.64 us (1%)
    pallas_call x1, Pallas kernels, shards(): pl.pallas_call(kernel, out_shape=(out, out), in_specs=[pl.BlockSpec(memor...  42.5 us

profile of v6, /device:TPU:1, one launch (start us, length us, event | category | flops | bytes accessed | tf_op | source)
XLA Modules:
  0.0 43.8 jit_solution(16389401096743052031)
XLA Ops:
  0.6 42.5 %shard_map.77 = (f32[128,256]{1,0:T(8,128)S(1)}, f32[128,256]{1,0:T(8,128)S(1)}) custom-call(bf16[128,256]{1,0:T(8,128)(2,1)} %q_own.1, bf16[128,256]{1,0:T(8,128)(2,1)} %c_own.1, s32[256,256]{1,0:T(8,128)} %mask_hbm.1, s32[256,128]{1,0:T(8,128)} %bitcast.3, s32[256,128]{1,0:T(8,128)} %bitcast.4, f32[4,128]{1,0:T(4,128)} %bitcast.5), custom_call_target="tpu_custom_call" | custom-call | tf_op jit(solution)/shard_map/pallas_call | solution.py:475
  43.1 0.7 %broadcast_multiply_fusion = (f32[128,256]{1,0:T(8,128)}, f32[128,256]{1,0:T(8,128)}) fusion(f32[128,256]{1,0:T(8,128)S(1)} %get-tuple-element.5, f32[128,256]{1,0:T(8,128)S(1)} %get-tuple-element.4), kind=kLoop, calls=%fused_computation | loop fusion | flops 65536 | bytes 524288 | tf_op jit(solution)/shard_map/mul | solution.py:493

commit v7 on v6

--- a/solution.py
+++ b/solution.py
@@ -244,10 +244,10 @@
     for i, dz in ((3, 1), (5, -3), (6, 3), (4, 4)):
         q_arrived(i, dz)
     q_pass(1)
+    wave(0, 8, 12)
+    wave(1, 8, 12)
     c_wait(2)
-    wave(2, 0, 8)
-    for g in range(3):
-        wave(g, 8, 12)
+    wave(2, 0, 12)
     q_passed(1)
     for g in range(3):
         wave(g, 12, 16)

time: 43.9 us -> 44.2 us (level)
  no operation moved by 1% of the time
where the time goes in v7:
time: 44.2 us; the launch traced here: 44.1 us
  Pallas kernels  42.8 us (97%)
  other arithmetic  0.72 us (2%)
  between operations  0.64 us (1%)
    pallas_call x1, Pallas kernels, shards(): pl.pallas_call(kernel, out_shape=(out, out), in_specs=[pl.BlockSpec(memor...  42.8 us

profile of v7, /device:TPU:1, one launch (start us, length us, event | category | flops | bytes accessed | tf_op | source)
XLA Modules:
  0.0 44.1 jit_solution(1949199668287778216)
XLA Ops:
  0.6 42.8 %shard_map.77 = (f32[128,256]{1,0:T(8,128)S(1)}, f32[128,256]{1,0:T(8,128)S(1)}) custom-call(bf16[128,256]{1,0:T(8,128)(2,1)} %q_own.1, bf16[128,256]{1,0:T(8,128)(2,1)} %c_own.1, s32[256,256]{1,0:T(8,128)} %mask_hbm.1, s32[256,128]{1,0:T(8,128)} %bitcast.3, s32[256,128]{1,0:T(8,128)} %bitcast.4, f32[4,128]{1,0:T(4,128)} %bitcast.5), custom_call_target="tpu_custom_call" | custom-call | tf_op jit(solution)/shard_map/pallas_call | solution.py:475
  43.4 0.7 %broadcast_multiply_fusion = (f32[128,256]{1,0:T(8,128)}, f32[128,256]{1,0:T(8,128)}) fusion(f32[128,256]{1,0:T(8,128)S(1)} %get-tuple-element.5, f32[128,256]{1,0:T(8,128)S(1)} %get-tuple-element.4), kind=kLoop, calls=%fused_computation | loop fusion | flops 65536 | bytes 524288 | tf_op jit(solution)/shard_map/mul | solution.py:493
